TPU v7x, 128 devices: a whole 4x4x4 slice. The times are simulated.
128 devices in a mesh: stream: 32 (over z, y, core), azim: 4 (over x).
Axes of the slice: x: 4, y: 4, z: 4, core: 2. Of those that a mesh axis runs over, the one named last changes fastest.
Arguments:
- history: float32 [3, 3, 64, 262144], P(None, None, None, ('stream', 'azim')), may hold values from -6 to 6
- block_ids: int32 [16384], P(('stream', 'azim')), may hold values from 0 to 16383, as said below
- len_axial: float32 [128], replicated, may hold values from 0.7 to 17.5, as said below
- len_azim: float32 [16], replicated, may hold values from 0.8 to 2.4
- len_radial: float32 [128], replicated, may hold values from 0.8 to 2.4
- solid: int32 [128, 16, 128], P('stream', 'azim'), may hold values 0 or 1
Outputs:
- velocity: float32 [3, 4, 4, 4, 128, 16, 128], P(None, None, None, None, 'stream', 'azim')
- pressure: float32 [4, 4, 4, 128, 16, 128], P(None, None, None, 'stream', 'azim')
Inputs may be any that keep to these rules, and one draw needn't show every extreme that they name: `block_ids`: A permutation of 0 .. 16383. Block id g goes to the device of linear index g // 128 (flow index major), which lies in the sender's azimuthal sector. A device sends at most 2 blocks to any other device; in every draw some device sends 2 blocks to some other, and some device receives 2 blocks from every other device of its sector. `len_axial`: Positive.
All inputs are finite; a program needn't handle non-finite values. No bound on the sum of `solid` on one device may be relied on, other than what follows from the above.
Results may differ from a plain program's by a relative error of at most 0.0001.
Values sent between devices are 32-bit elements; how exact they have to be, the bound alone decides.
No kernel may reach another device: no remote copies, remote signals or barrier semaphores. Data moves between devices by JAX's collectives and lax.ppermute only.
A program may use at most 128 MiB of HBM per device.

v0:
```python
import math

import jax
import jax.numpy as jnp
import numpy as np
from jax import lax
from jax.sharding import PartitionSpec as P

CAP = 2
ITERS = 2


DT = 0.01
PENALTY = 100.0
HIGH = lax.Precision.HIGHEST
FORWARD = ("ia,kabc...->kibc...", "ib,kabc...->kaic...", "ic,kabc...->kabi...")
BACKWARD = ("ai,kabc...->kibc...", "bi,kabc...->kaic...", "ci,kabc...->kabi...")


def extended(cells, sides, width):
    for axis, dim in sides:
        count = lax.axis_size(axis)
        head = lax.slice_in_dim(cells, 0, width, axis=dim)
        tail = lax.slice_in_dim(cells, cells.shape[dim] - width, cells.shape[dim], axis=dim)
        cells = jnp.concatenate(
            [
                lax.ppermute(tail, axis, [(i, (i + 1) % count) for i in range(count)]),
                cells,
                lax.ppermute(head, axis, [((i + 1) % count, i) for i in range(count)]),
            ],
            axis=dim,
        )
    return cells


def node_tables():
    root = 1.0 / math.sqrt(5.0)
    points = np.array([-1.0, -root, root, 1.0])
    weights = np.array([1.0 / 6.0, 5.0 / 6.0, 5.0 / 6.0, 1.0 / 6.0])
    legendre = (5.0 * points**3 - 3.0 * points) / 2.0
    slope = np.zeros((4, 4))
    for first in range(4):
        for second in range(4):
            if first != second:
                slope[first, second] = legendre[first] / (
                    legendre[second] * (points[first] - points[second])
                )
    slope[0, 0] = -3.0
    slope[3, 3] = 3.0
    return (jnp.asarray(slope, dtype=jnp.float32), jnp.asarray(weights, dtype=jnp.float32))


def along(field, axis_pick, backward):
    slope, _ = node_tables()
    form = BACKWARD[axis_pick] if backward else FORWARD[axis_pick]
    return jnp.einsum(form, slope, field, precision=HIGH)


def weight_cube(trailing):
    _, weights = node_tables()
    cube = weights[:, None, None] * weights[None, :, None] * weights[None, None, :]
    return cube.reshape((4, 4, 4) + (1,) * trailing)


def predictor(history, scales):
    newest, middle, oldest = (history[0], history[1], history[2])
    extrap = 3.0 * newest - 3.0 * middle + oldest
    advect = jnp.zeros_like(extrap)
    for axis_pick in range(3):
        advect = advect + extrap[axis_pick] * (scales[axis_pick] * along(extrap, axis_pick, False))
    return 3.0 * newest - 1.5 * middle + oldest / 3.0 - DT * advect


def load_elements(predicted, scales):
    trailing = predicted.ndim - 4
    jacobian = 1.0 / (scales[0] * scales[1] * scales[2])
    spread = jnp.zeros_like(predicted[0])
    for axis_pick in range(3):
        spread = (
            spread
            + scales[axis_pick] * along(predicted[axis_pick : axis_pick + 1], axis_pick, False)[0]
        )
    return -(jacobian * weight_cube(trailing)) * spread


def stiffness(field, scales):
    trailing = field.ndim - 3
    jacobian = 1.0 / (scales[0] * scales[1] * scales[2])
    cube = weight_cube(trailing)
    lifted = field[None]
    total = jnp.zeros_like(lifted)
    for axis_pick in range(3):
        factor = scales[axis_pick] * scales[axis_pick] * jacobian * cube
        total = total + along(factor * along(lifted, axis_pick, False), axis_pick, True)
    return total[0]


def gradient(field, scales):
    lifted = field[None]
    return jnp.concatenate(
        [scales[axis_pick] * along(lifted, axis_pick, False) for axis_pick in range(3)], axis=0
    )


def assemble(partial_value, slab_at, slab_count):
    ex_count = partial_value.shape[3]
    low_face = partial_value[:, :, 0]
    high_face = partial_value[:, :, 3]
    zero_layer = jnp.zeros_like(high_face[..., :1])
    below = jnp.concatenate([zero_layer, high_face[..., :-1]], axis=-1)
    above = jnp.concatenate([low_face[..., 1:], zero_layer], axis=-1)
    radial_end = jnp.arange(high_face.shape[-1]) == high_face.shape[-1] - 1
    new_high = jnp.where(radial_end, 0.0, high_face + above)
    summed = jnp.concatenate(
        [(low_face + below)[:, :, None], partial_value[:, :, 1:3], new_high[:, :, None]], axis=2
    )
    framed = extended(summed, (("stream", 3), ("azim", 4)), 1)
    low_face = framed[:, 0]
    high_face = framed[:, 3]
    new_low = low_face[:, :, :, 1:-1] + high_face[:, :, :, :-2]
    new_high = high_face[:, :, :, 1:-1] + low_face[:, :, :, 2:]
    sector_sum = jnp.concatenate(
        [new_low[:, None], framed[:, 1:3, :, :, 1:-1], new_high[:, None]], axis=1
    )
    low_face = sector_sum[0]
    high_face = sector_sum[3]
    inlet = (jnp.arange(ex_count) == 0)[:, None, None] & (slab_at == 0)
    lower = jnp.where(inlet, 0.0, high_face[:, :, :-2])
    outlet = (jnp.arange(ex_count) == ex_count - 1)[:, None, None] & (slab_at == slab_count - 1)
    new_low = low_face[:, :, 1:-1] + lower
    new_high = jnp.where(outlet, 0.0, high_face[:, :, 1:-1] + low_face[:, :, 2:])
    return jnp.concatenate([new_low[None], sector_sum[1:3, :, :, 1:-1], new_high[None]], axis=0)


def owned_inner(first, second):
    owned = (jnp.arange(4) < 3).astype(jnp.float32)
    weight = (owned[:, None, None] * owned[None, :, None] * owned[None, None, :]).reshape(
        4, 4, 4, 1, 1, 1
    )
    return jnp.sum(weight * first * second)


def body(history, block_ids, len_axial, len_azim, len_radial, solid):
    ex_count, ey_count, ez_count = solid.shape
    slots = block_ids.shape[0]
    width = history.shape[3] // slots
    slab_count = lax.axis_size("stream")
    sector_count = lax.axis_size("azim")
    slab_at = lax.axis_index("stream")
    sector_at = lax.axis_index("azim")
    owner = block_ids // slots
    target = owner // sector_count
    new_slot = block_ids % slots
    moving = target != slab_at
    peers = jnp.arange(slab_count, dtype=jnp.int32)
    onehot = (target[:, None] == peers[None, :]).astype(jnp.int32)
    earlier = jnp.cumsum(onehot, axis=0) - onehot
    ranked = jnp.sum(earlier * onehot, axis=1)
    lanes = slab_count * CAP
    place = jnp.where(moving, target * CAP + ranked, lanes)
    picked = (
        jnp.full((lanes,), slots, jnp.int32)
        .at[place]
        .set(jnp.arange(slots, dtype=jnp.int32), mode="drop")
    )
    labels = jnp.where(picked < slots, jnp.take(new_slot, jnp.minimum(picked, slots - 1)) + 1, 0)
    keep_at = jnp.where(moving, slots, new_slot)
    local_scales = (
        (2.0 / lax.dynamic_slice_in_dim(len_axial, slab_at * ex_count, ex_count))[:, None, None],
        (2.0 / lax.dynamic_slice_in_dim(len_azim, sector_at * ey_count, ey_count))[None, :, None],
        (2.0 / len_radial)[None, None, :],
    )
    data = history.reshape(9, 64, slots * width)
    leading = data.shape[:2]
    blocks = data.reshape(leading + (slots, width))
    padded = jnp.concatenate([blocks, jnp.zeros(leading + (1, width), data.dtype)], axis=2)
    outgoing = jnp.take(padded, picked, axis=2).reshape(leading + (lanes * width,))
    marks = labels.astype(jnp.float32).reshape(1, 1, lanes)
    outgoing, marks, blocks = (outgoing, marks, blocks)
    arrived, landed = (
        lax.all_to_all(outgoing, "stream", split_axis=2, concat_axis=2, tiled=True),
        lax.all_to_all(marks, "stream", split_axis=2, concat_axis=2, tiled=True),
    )
    leading = blocks.shape[:2]
    landing = landed.reshape(lanes).astype(jnp.int32)
    where_to = jnp.where(landing > 0, landing - 1, slots)
    result = jnp.zeros(leading + (slots + 1, width), blocks.dtype)
    result = result.at[:, :, keep_at].set(blocks)
    result = result.at[:, :, where_to].set(arrived.reshape(leading + (lanes, width)))
    local = (
        result[:, :, :slots]
        .reshape(leading + (slots * width,))
        .reshape(3, 3, 4, 4, 4, ex_count, ey_count, ez_count)
    )
    numer = predictor(local, local_scales)
    predicted = numer / (11.0 / 6.0 + DT * PENALTY * solid.astype(jnp.float32))
    load = assemble(load_elements(predicted, local_scales), slab_at, slab_count)
    solution = jnp.zeros_like(load)
    residual = load

    def squares(field):
        return lax.psum(owned_inner(field, field), ("stream", "azim"))

    direction = load
    norm_now = squares(residual)
    for step in range(ITERS):
        image = assemble(stiffness(direction, local_scales), slab_at, slab_count)
        alpha = norm_now / lax.psum(owned_inner(direction, image), ("stream", "azim"))
        solution = solution + alpha * direction
        if step + 1 < ITERS:
            residual = residual - alpha * image
            norm_next = squares(residual)
            direction = residual + norm_next / norm_now * direction
            norm_now = norm_next
    velocity = predicted - gradient(solution, local_scales)
    return (velocity, solution)


def solution(mesh):
    in_specs = (
        P(None, None, None, ("stream", "azim")),
        P(("stream", "azim")),
        P(),
        P(),
        P(),
        P("stream", "azim", None),
    )
    out_specs = (
        P(None, None, None, None, "stream", "azim", None),
        P(None, None, None, "stream", "azim", None),
    )
    return jax.shard_map(body, mesh=mesh, in_specs=in_specs, out_specs=out_specs, check_vma=False)
```

profile of v0, /device:TPU:1, one launch (start us, length us, event | category | flops | bytes accessed | tf_op | source)
XLA Modules:
  0.0 528.2 jit_solution(9133871971020760954)
XLA Ops:
  4.3 9.6 %all-to-all-start = ((f32[1,1,64]{1,0,2:T(1,128)}), f32[1,1,64]{1,0,2:T(1,128)S(1)}, u32[]{:S(2)}, u32[]{:S(2)}) async-start(f32[1,1,64]{1,0,2:T(1,128)} %copy.262), calls=%async_computation | async-start | bytes 65536 | tf_op jit(solution)/shard_map/all_to_all | solution.py:182
  13.9 8.0 %copy.260 = f32[3,3,64,2048]{2,3,1,0:T(8,128)} copy(f32[3,3,64,2048]{3,2,1,0:T(8,128)} %param.30) | data formatting | bytes 9437184 | tf_op args[0]
  22.0 8.2 %concatenate.85 = f32[9,64,129,16]{1,3,2,0:T(8,128)} pad(f32[9,64,128,16]{1,3,2,0:T(8,128)} %bitcast.323, f32[]{:T(128)} %constant.58.clone.1), padding=0_0x0_0x0_1x0_0 | pad | bytes 9474052 | tf_op jit(solution)/shard_map/concatenate | solution.py:176
  30.1 6.8 %gather_fusion.1 = f32[64,9,64,16]{2,3,1,0:T(8,128)} fusion(f32[9,64,129,16]{1,3,2,0:T(8,128)} %concatenate.85, s32[1024]{0:T(1024)S(1)} %get-tuple-element.87), kind=kCustom, calls=%fused_computation.1 | custom fusion | bytes 4718848 | tf_op jit(solution)/shard_map/jit(_take)/gather | solution.py:177
  36.9 4.9 copy.263
  42.0 2.8 bitcast_select_fusion
  44.8 6.2 %copy.483 = f32[9,64,1024]{1,0,2:T(8,128)} copy(f32[9,64,1024]{1,2,0:T(8,128)S(1)} %bitcast_select_fusion) | data formatting | bytes 4718592 | tf_op jit(solution)/shard_map/jit(_take)/select_n | solution.py:177
  51.0 7.4 %reshape.534 = f32[32,1,18432]{2,1,0:T(1,128)} reshape(f32[1024,9,64]{2,1,0:T(8,128)} %bitcast.325) | data formatting | bytes 4718592
  58.3 8.0 %all-to-all-start.1 = ((f32[32,1,18432]{2,1,0:T(1,128)}), f32[32,1,18432]{2,1,0:T(1,128)S(1)}, u32[]{:S(2)}, u32[]{:S(2)}) async-start(f32[32,1,18432]{2,1,0:T(1,128)} %reshape.534), calls=%async_computation.1 | async-start | bytes 4718592 | tf_op jit(solution)/shard_map/all_to_all | solution.py:181
  66.3 7.8 %copy.261 = f32[128,9,64,16]{2,3,1,0:T(8,128)} copy(f32[128,9,64,16]{2,3,0,1:T(8,128)} %bitcast.324) | data formatting | bytes 9437184 | tf_op jit(solution)/shard_map/reshape;reshape | solution.py:175
  74.2 4.3 broadcast_in_dim.195
  78.5 25.0 %scatter_fusion = f32[9,64,129,16]{1,3,2,0:T(8,128)} fusion(f32[9,64,129,16]{1,3,2,0:T(8,128)} %broadcast_in_dim.195, s32[128]{0:T(128)S(1)} %get-tuple-element.21, f32[128,9,64,16]{2,3,1,0:T(8,128)} %copy.261), kind=kCustom, calls=%fused_computation.2 | custom fusion | bytes 14156288 | tf_op jit(solution)/shard_map/scatter | solution.py:188
  106.3 8.3 %reduce.2 = f32[32,18432]{1,0:T(8,128)} reduce(f32[32,1,18432]{2,1,0:T(1,128)S(1)} %all-to-all-done.1, f32[]{:T(128)} %broadcast.582), dimensions={1}, to_apply=%all_to_all.7.reduce_sub_computation | reduce | bytes 4718596 | tf_op jit(solution)/shard_map/all_to_all | solution.py:181
  114.6 6.3 %reshape.535 = f32[1024,9,64]{2,1,0:T(8,128)} reshape(f32[32,18432]{1,0:T(8,128)} %reduce.2) | data formatting | bytes 4718592
  120.9 7.8 %copy.266 = f32[64,9,64,16]{2,3,1,0:T(8,128)} copy(f32[64,9,64,16]{2,1,3,0:T(8,128)} %bitcast.326) | data formatting | bytes 4718592 | tf_op jit(solution)/shard_map/reshape | solution.py:189
  128.7 13.1 %scatter_fusion.1 = f32[9,64,129,16]{1,3,2,0:T(8,128)} fusion(f32[9,64,129,16]{1,3,2,0:T(8,128)} %scatter_fusion, s32[64]{0:T(128)S(1)} %fusion.89, f32[64,9,64,16]{2,3,1,0:T(8,128)} %copy.266), kind=kCustom, calls=%fused_computation.4 | custom fusion | bytes 7078144 | tf_op jit(solution)/shard_map/scatter | solution.py:189
  141.8 6.4 %subtract_add_fusion = (f32[3,64,128,16]{1,3,2,0:T(8,128)S(1)}, f32[3,64,128,16]{1,3,2,0:T(8,128)}) fusion(f32[9,64,129,16]{1,3,2,0:T(8,128)} %scatter_fusion.1), kind=kLoop, calls=%fused_computation.7 | loop fusion | flops 3145728 | bytes 7864320 | tf_op jit(solution)/shard_map/add | solution.py:67
  148.2 10.7 %copy.270 = f32[3,64,128,16]{3,2,1,0:T(8,128)} copy(f32[3,64,128,16]{1,3,2,0:T(8,128)S(1)} %get-tuple-element.24) | data formatting | bytes 3145728 | tf_op jit(solution)/shard_map/add | solution.py:67
  158.9 9.2 %add.217 = f32[3,4,4,4,4,4,128]{6,5,4,3,2,1,0:T(4,128)} reshape(f32[3,64,128,16]{3,2,1,0:T(8,128)} %copy.270) | data formatting | bytes 3145728 | tf_op jit(solution)/shard_map/add | solution.py:67
  168.1 5.8 %fusion.5 = f32[3,4,4,4,4,128,4]{5,6,4,3,2,1,0:T(4,128)} fusion(f32[4,4,1,1,1,1,1]{1,0,6,5,4,3,2:T(4,128)S(1)} %copy-done.20, f32[3,4,4,4,4,4,128]{6,5,4,3,2,1,0:T(4,128)} %add.217), kind=kOutput, calls=%fused_computation.19 | convolution fusion | flops 18874368 | bytes 3145792 | tf_op jit(solution)/shard_map/ic,kabc...->kabi.../dot_general | solution.py:56
  173.8 4.2 fusion.7
  178.1 1.8 fusion.96
  179.9 5.7 %copy.268 = f32[1,64,128,16]{3,2,1,0:T(8,128)} copy(f32[1,64,128,16]{1,3,2,0:T(8,128)} %get-tuple-element.26) | data formatting | bytes 1048576 | tf_op jit(solution)/shard_map/slice | solution.py:70
  185.5 3.3 mul.728
  190.1 4.5 copy.272
  194.6 3.3 mul.735
  199.1 4.5 copy.276
  203.6 4.2 mul.742
  207.8 2.2 copy.277
  210.0 10.5 %copy.267 = f32[3,64,128,16]{3,2,1,0:T(8,128)} copy(f32[3,64,128,16]{1,3,2,0:T(8,128)S(1)} %copy-done.2) | data formatting | bytes 3145728 | tf_op jit(solution)/shard_map/add | solution.py:71
  220.5 9.3 %add.214 = f32[3,4,4,4,4,4,128]{6,5,4,3,2,1,0:T(4,128)} reshape(f32[3,64,128,16]{3,2,1,0:T(8,128)} %copy.267) | data formatting | bytes 3145728 | tf_op jit(solution)/shard_map/add | solution.py:71
  229.8 10.5 %fusion.3 = f32[3,4,4,4,4,4,128]{6,1,5,4,3,2,0:T(4,128)S(1)} fusion(f32[3,4,4,4,4,4,128]{6,5,4,3,2,1,0:T(4,128)} %add.214, f32[3,4,4,4,4,128,4]{5,6,4,3,2,1,0:T(4,128)} %fusion.5, f32[3,4,4,4,4,128,4]{5,6,4,3,2,1,0:T(4,128)} %fusion.7, f32[4,4,1,1,1,1,1]{1,0,6,5,4,3,2:T(4,128)S(1)} %copy-done.20, f32[3,4,4,4,4,4,128]{6,5,4,3,2,1,0:T(4,128)S(1)} %copy-done.1, ...), kind=kOutput, calls=%fused_computation.14 | convolution fusion | flops 23199744 | bytes 9445984 | tf_op jit(solution)/shard_map/ia,kabc...->kibc.../dot_general | solution.py:56
  242.3 1.3 fusion.63
  243.7 1.6 fusion.16
  246.0 1.8 collective-permute-start
  247.8 1.9 collective-permute-done
  249.7 2.7 collective-permute-done.1
  252.6 1.7 collective-permute-start.2
  255.5 2.9 collective-permute-done.2
  261.3 1.3 fusion.55
  262.6 1.3 fusion.59
  264.0 1.3 fusion.18
  267.1 1.3 fusion.53
  268.5 1.3 fusion.57
  270.6 2.3 collective-permute-start.4
  273.0 1.9 collective-permute-done.4
  274.9 2.4 collective-permute-done.5
  279.0 2.7 collective-permute-start.7
  282.4 1.4 copy.360
  288.1 69.8 %all-reduce.7 = (f32[]{:T(128)}, f32[]{:T(128)}) all-reduce(f32[]{:T(128)} %get-tuple-element.11, f32[]{:T(128)} %get-tuple-element.10), channel_id=1, replica_groups=mesh['stream'=32,'azim'=4] {'stream','azim'}, use_global_device_ids=true, to_apply=%region_6.7 | all-reduce | flops 2 | bytes 16 | tf_op jit(solution)/shard_map/psum | solution.py:202
  359.3 2.0 fusion.32
  361.2 62.9 %psum.30 = f32[]{:T(128)} all-reduce(f32[]{:T(128)} %fusion.32), channel_id=1, replica_groups=mesh['stream'=32,'azim'=4] {'stream','azim'}, use_global_device_ids=true, to_apply=%region_10.11 | all-reduce | flops 1 | bytes 8 | tf_op jit(solution)/shard_map/psum | solution.py:202
  426.2 1.3 fusion.46
  427.5 1.3 fusion.50
  430.6 1.3 fusion.44
  431.9 1.3 fusion.48
  435.1 1.7 collective-permute-start.8
  436.8 1.9 collective-permute-done.8
  438.8 2.7 collective-permute-done.9
  442.1 2.7 collective-permute-start.11
  444.8 3.0 collective-permute-done.10
  450.0 68.5 %psum.31 = f32[]{:T(128)} all-reduce(f32[]{:T(128)} %fusion.35), channel_id=1, replica_groups=mesh['stream'=32,'azim'=4] {'stream','azim'}, use_global_device_ids=true, to_apply=%region_12.13 | all-reduce | flops 1 | bytes 8 | tf_op jit(solution)/shard_map/psum | solution.py:208
  520.3 1.3 fusion.42
  526.4 1.6 copy.339
  (175 shorter events, 37.1 us)
Async XLA Ops:
  4.3 54.1 %all-to-all-start = ((f32[1,1,64]{1,0,2:T(1,128)}), f32[1,1,64]{1,0,2:T(1,128)S(1)}, u32[]{:S(2)}, u32[]{:S(2)}) async-start(f32[1,1,64]{1,0,2:T(1,128)} %copy.262), calls=%async_computation | async-start | bytes 65536 | tf_op jit(solution)/shard_map/all_to_all | solution.py:182
  58.3 47.4 %all-to-all-start.1 = ((f32[32,1,18432]{2,1,0:T(1,128)}), f32[32,1,18432]{2,1,0:T(1,128)S(1)}, u32[]{:S(2)}, u32[]{:S(2)}) async-start(f32[32,1,18432]{2,1,0:T(1,128)} %reshape.534), calls=%async_computation.1 | async-start | bytes 4718592 | tf_op jit(solution)/shard_map/all_to_all | solution.py:181
  78.4 25.0 %copy-start.31 = (f32[128]{0:T(128)S(1)}, f32[128]{0:T(128)}, u32[]{:S(2)}) copy-start(f32[128]{0:T(128)} %param.32) | copy-start | bytes 1540
  78.5 25.0 %copy-start.32 = (f32[16]{0:T(128)S(1)}, f32[16]{0:T(128)}, u32[]{:S(2)}) copy-start(f32[16]{0:T(128)} %param.33) | copy-start | bytes 196
  78.5 25.1 %copy-start.33 = (f32[128]{0:T(128)S(1)}, f32[128]{0:T(128)}, u32[]{:S(2)}) copy-start(f32[128]{0:T(128)} %param.34) | copy-start | bytes 1540
  78.5 25.1 %copy-start.25 = (f32[4]{0:T(128)S(1)}, f32[4]{0:T(128)}, u32[]{:S(2)}) copy-start(f32[4]{0:T(128)} %constant.125.clone) | copy-start | bytes 52
  78.5 25.4 %copy-start.19 = (s32[4,4,128]{2,1,0:T(4,128)S(1)}, s32[4,4,128]{2,1,0:T(4,128)}, u32[]{:S(2)}) copy-start(s32[4,4,128]{2,1,0:T(4,128)} %param.35) | copy-start | bytes 24580
  103.5 142.3 %copy-start.26 = (pred[128]{0:T(512)(128)(4,1)}, pred[128]{0:T(512)(128)(4,1)S(1)}, u32[]{:S(2)}) copy-start(pred[128]{0:T(512)(128)(4,1)S(1)} %iota_compare_fusion.5) | copy-start | bytes 388
  103.6 140.1 %copy-start.21 = (f32[4]{0:T(128)}, f32[4]{0:T(128)S(1)}, u32[]{:S(2)}) copy-start(f32[4]{0:T(128)S(1)} %get-tuple-element.90) | copy-start | bytes 52
  103.6 140.1 %copy-start.23 = (f32[4]{0:T(128)}, f32[4]{0:T(128)S(1)}, u32[]{:S(2)}) copy-start(f32[4]{0:T(128)S(1)} %get-tuple-element.16) | copy-start | bytes 52
  103.6 140.0 %copy-start.29 = (f32[128]{0:T(128)}, f32[128]{0:T(128)S(1)}, u32[]{:S(2)}) copy-start(f32[128]{0:T(128)S(1)} %get-tuple-element.20) | copy-start | bytes 1540
  158.9 9.2 %copy-start.20 = (f32[4,4,1,1,1,1,1]{1,0,6,5,4,3,2:T(4,128)S(1)}, f32[4,4,1,1,1,1,1]{1,0,6,5,4,3,2:T(4,128)}, u32[]{:S(2)}) copy-start(f32[4,4,1,1,1,1,1]{1,0,6,5,4,3,2:T(4,128)} %constant.141) | copy-start | bytes 196
  168.1 5.8 %copy-start = (f32[3,4,4,4,4,4,128]{6,5,4,3,2,1,0:T(4,128)S(1)}, f32[3,4,4,4,4,4,128]{6,5,4,3,2,1,0:T(4,128)}, u32[]{:S(2)}) copy-start(f32[3,4,4,4,4,4,128]{6,5,4,3,2,1,0:T(4,128)} %add.217) | copy-start | bytes 4718596
  188.9 1.2 copy-start.4
  197.9 1.2 copy-start.3
  203.6 6.4 %copy-start.2 = (f32[3,64,128,16]{1,3,2,0:T(8,128)S(1)}, f32[3,64,128,16]{1,3,2,0:T(8,128)}, u32[]{:S(2)}) copy-start(f32[3,64,128,16]{1,3,2,0:T(8,128)} %get-tuple-element.25) | copy-start | bytes 4718596
  220.5 9.3 %copy-start.1 = (f32[3,4,4,4,4,4,128]{6,5,4,3,2,1,0:T(4,128)S(1)}, f32[3,4,4,4,4,4,128]{6,5,4,3,2,1,0:T(4,128)}, u32[]{:S(2)}) copy-start(f32[3,4,4,4,4,4,128]{6,5,4,3,2,1,0:T(4,128)} %add.217) | copy-start | bytes 4718596
  240.3 0.7 copy-start.7
  246.0 3.8 collective-permute-start
  247.8 4.7 collective-permute-start.1
  252.6 5.8 %collective-permute-start.2 = (f32[4,4,4,6,1,128]{5,0,4,3,2,1:T(4,128)S(1)}, f32[4,4,4,6,1,128]{5,0,4,3,2,1:T(4,128)S(1)}, u32[]{:S(2)}, u32[]{:S(2)}) collective-permute-start(f32[4,4,4,6,1,128]{5,0,4,3,2,1:T(4,128)S(1)} %get-tuple-element.51), channel_id=1, source_target_pairs={{0,1},{1,2},{2,3},{3,0},{4,5},{5,6},{6,7},{7,4},{8,9},{9,10},{10,1... | collective-permute-start | bytes 589832 | tf_op jit(solution)/shard_map/ppermute | solution.py:27
  254.2 5.4 %collective-permute-start.3 = (f32[4,4,4,6,1,128]{5,0,4,3,2,1:T(4,128)S(1)}, f32[4,4,4,6,1,128]{5,0,4,3,2,1:T(4,128)S(1)}, u32[]{:S(2)}, u32[]{:S(2)}) collective-permute-start(f32[4,4,4,6,1,128]{5,0,4,3,2,1:T(4,128)S(1)} %get-tuple-element.52), channel_id=1, source_target_pairs={{1,0},{2,1},{3,2},{0,3},{5,4},{6,5},{7,6},{4,7},{9,8},{10,9},{11,1... | collective-permute-start | bytes 589832 | tf_op jit(solution)/shard_map/ppermute | solution.py:29
  255.5 5.1 copy-start.16
  261.0 3.0 copy-start.14
  264.0 2.4 copy-start.9
  264.0 2.4 copy-start.11
  269.8 0.6 copy-start.27
  270.6 4.3 collective-permute-start.4
  273.0 4.4 collective-permute-start.5
  277.3 0.7 copy-start.5
  279.0 6.0 %collective-permute-start.6 = (f32[4,4,4,6,1,128]{5,4,3,2,0,1:T(1,128)}, f32[4,4,4,6,1,128]{5,4,3,2,0,1:T(1,128)}, u32[]{:S(2)}, u32[]{:S(2)}) collective-permute-start(f32[4,4,4,6,1,128]{5,4,3,2,0,1:T(1,128)} %get-tuple-element.47), channel_id=1, source_target_pairs={{0,1},{1,2},{2,3},{3,0},{4,5},{5,6},{6,7},{7,4},{8,9},{9,10},{10,1... | collective-permute-start | bytes 589832 | tf_op jit(solution)/shard_map/ppermute | solution.py:27
  279.0 6.0 %collective-permute-start.7 = (f32[4,4,4,6,1,128]{5,4,3,2,0,1:T(1,128)}, f32[4,4,4,6,1,128]{5,4,3,2,0,1:T(1,128)}, u32[]{:S(2)}, u32[]{:S(2)}) collective-permute-start(f32[4,4,4,6,1,128]{5,4,3,2,0,1:T(1,128)} %get-tuple-element.48), channel_id=1, source_target_pairs={{1,0},{2,1},{3,2},{0,3},{5,4},{6,5},{7,6},{4,7},{9,8},{10,9},{11,1... | collective-permute-start | bytes 589832 | tf_op jit(solution)/shard_map/ppermute | solution.py:29
  283.8 2.6 copy-start.6
  286.2 0.6 copy-start.17
  286.2 0.7 copy-start.13
  425.5 3.3 copy-start.15
  426.2 3.7 copy-start.10
  426.2 3.7 copy-start.12
  434.3 0.6 copy-start.28
  435.1 3.6 collective-permute-start.8
  436.8 4.7 collective-permute-start.9
  441.8 6.0 %collective-permute-start.10 = (f32[4,4,4,6,1,128]{5,4,3,2,0,1:T(1,128)S(1)}, f32[4,4,4,6,1,128]{5,4,3,2,0,1:T(1,128)S(1)}, u32[]{:S(2)}, u32[]{:S(2)}) collective-permute-start(f32[4,4,4,6,1,128]{5,4,3,2,0,1:T(1,128)S(1)} %get-tuple-element.41), channel_id=1, source_target_pairs={{0,1},{1,2},{2,3},{3,0},{4,5},{5,6},{6,7},{7,4},{8,9},{9,10},{10,1... | collective-permute-start | bytes 589832 | tf_op jit(solution)/shard_map/ppermute | solution.py:27
  442.1 5.7 %collective-permute-start.11 = (f32[4,4,4,6,1,128]{5,4,3,2,0,1:T(1,128)S(1)}, f32[4,4,4,6,1,128]{5,4,3,2,0,1:T(1,128)S(1)}, u32[]{:S(2)}, u32[]{:S(2)}) collective-permute-start(f32[4,4,4,6,1,128]{5,4,3,2,0,1:T(1,128)S(1)} %get-tuple-element.42), channel_id=1, source_target_pairs={{1,0},{2,1},{3,2},{0,3},{5,4},{6,5},{7,6},{4,7},{9,8},{10,9},{11,1... | collective-permute-start | bytes 589832 | tf_op jit(solution)/shard_map/ppermute | solution.py:29
  448.2 0.6 copy-start.18
  448.3 0.7 copy-start.8
  519.9 3.1 copy-start.24
  521.6 3.3 copy-start.22
  523.0 2.3 copy-start.30
where the time goes:
time: 536 us; the launch traced here: 528 us
  blocking collectives  201 us (38%)
  local copies, waits for them, and re-layouts  188 us (35%)
  matrix products  43.3 us (8%)
  other arithmetic  35.3 us (7%)
  starting transfers between devices  31.9 us (6%)
  waiting for transfers between devices  22.1 us (4%)
  between operations  5.85 us (1%)
    psum x2, blocking collectives, squares(): return lax.psum(owned_inner(field, field), ('stream', 'azim'))  133 us
    psum x1, blocking collectives, body(): lax.psum(owned_inner(direction, image), ('stream', 'azim'))  68.5 us
    dot_general x21, matrix products, along(): return jnp.einsum(form, slope, field, precision=HIGH)  43.3 us
    unnamed x78, local copies, waits for them, and re-layouts  28.1 us
    scatter x1, local copies, waits for them, and re-layouts, body(): result = result.at[:, :, keep_at].set(blocks)  25 us
    add x2, local copies, waits for them, and re-layouts, predictor(): extrap = 3.0 * newest - 3.0 * middle + oldest  19.8 us
    add x2, local copies, waits for them, and re-layouts, predictor(): return 3.0 * newest - 1.5 * middle + oldest / 3.0 - DT * advect  19.8 us
    slice x4, local copies, waits for them, and re-layouts, predictor(): extrap[axis_pick] * (scales[axis_pick] * along(extrap, axis_pick, False))  16.5 us
  transfers between devices with their start and end apart: 14, of which 10 were waited for; matrix products, arithmetic and copies ran while one was open for 16% of the time, Pallas kernels for 0%

commit v1 on v0

v1 whole, which is shorter than its diff:
```python
import functools
import math

import jax
import jax.numpy as jnp
import numpy as np
from jax import lax
from jax.experimental import pallas as pl
from jax.experimental.pallas import tpu as pltpu
from jax.sharding import PartitionSpec as P

CAP = 2
DT = 0.01
PENALTY = 100.0
VMEM_LIMIT = 40 * 1024 * 1024
F32 = jnp.float32


def node_tables():
    root = 1.0 / math.sqrt(5.0)
    points = np.array([-1.0, -root, root, 1.0])
    weights = np.array([1.0 / 6.0, 5.0 / 6.0, 5.0 / 6.0, 1.0 / 6.0])
    legendre = (5.0 * points**3 - 3.0 * points) / 2.0
    slope = np.zeros((4, 4))
    for first in range(4):
        for second in range(4):
            if first != second:
                slope[first, second] = legendre[first] / (
                    legendre[second] * (points[first] - points[second])
                )
    slope[0, 0] = -3.0
    slope[3, 3] = 3.0
    return slope, weights


SLOPE, WEIGHT = node_tables()
STIFF = SLOPE.T @ np.diag(WEIGHT) @ SLOPE
EDGE = float(WEIGHT[0])

ROWS = 8
BLOCK_ROWS = 24
PEER_ROWS = CAP * BLOCK_ROWS + ROWS


def iotas():
    lane = lax.broadcasted_iota(jnp.int32, (ROWS, 128), 1)
    sub = lax.broadcasted_iota(jnp.int32, (ROWS, 128), 0)
    return lane, sub


def lanes(x, shift):
    shift %= 128
    return pltpu.roll(x, shift, 1) if shift else x


def subs(x, shift):
    shift %= ROWS
    return pltpu.roll(x, shift, 0) if shift else x


def combine(coefs, values):
    total = None
    for coef, value in zip(coefs, values):
        coef = float(coef)
        if coef == 0.0:
            continue
        term = coef * value
        total = term if total is None else total + term
    return total


def choose(key, values):
    result = values[0]
    for at in range(1, len(values)):
        result = jnp.where(key == at, values[at], result)
    return result


def swap_groups(tiles, group):
    turned = [lanes(tile, 16 * t) for t, tile in enumerate(tiles)]
    result = []
    for g in range(8):
        mixed = choose((group - g) & 7, turned)
        result.append(lanes(mixed, -16 * g))
    return result


def pack_kernel(ids, len_axial, len_azim, len_radial, hist, send, keep, count, table):
    sectors = lax.axis_size("azim")
    me = lax.axis_index("stream")
    step = pl.program_id(0)
    columns = hist.shape[1] // 128
    lane, sub = iotas()
    group = lane >> 4

    @pl.when(step == 0)
    def _():
        for t in range(send.shape[0] // PEER_ROWS):
            count[t] = 0
            send[pl.ds(t * PEER_ROWS + CAP * BLOCK_ROWS, ROWS), :] = jnp.zeros((ROWS, 128), F32)
        whole = jnp.broadcast_to(len_radial[...], (ROWS, 128))
        rows = choose(sub, [lanes(whole, -16 * z) for z in range(8)])
        rows = jnp.where(group == 0, rows, 0.0)
        for shift in (16, 32, 64):
            rows = rows + lanes(rows, shift)
        table[...] = rows

    def pattern(low, high):
        return jnp.where(sub < 4, F32(low), F32(high))

    def column(at, carry):
        offset = pl.multiple_of(at * 128, 128)

        def level(which, comp, t):
            return hist[pl.ds((which * 3 + comp) * 64 + 8 * t, ROWS), pl.ds(offset, 128)]

        places = []
        axial = azim = radial = None
        for piece in range(8):
            p = (step * columns + at) * 8 + piece
            ident = ids[p]
            owner = ident >> 7
            slot = ident & 127
            flow = owner // sectors
            sector = owner - flow * sectors
            places.append((flow, slot))
            one_axial = len_axial[flow * 4 + (slot >> 5)]
            one_azim = len_azim[sector * 4 + ((slot >> 3) & 3)]
            one_radial = table[pl.ds(slot & 7, 1), :]
            if piece == 0:
                axial = jnp.full((ROWS, 128), one_axial, F32)
                azim = jnp.full((ROWS, 128), one_azim, F32)
                radial = jnp.broadcast_to(one_radial, (ROWS, 128))
            else:
                axial = jnp.where(group == piece, one_axial, axial)
                azim = jnp.where(group == piece, one_azim, azim)
                radial = jnp.where(group == piece, one_radial, radial)
        scales = [(-2.0 * DT) / length for length in (axial, azim, radial)]

        extrap = [
            [3.0 * level(0, comp, t) - 3.0 * level(1, comp, t) + level(2, comp, t) for t in range(8)]
            for comp in range(3)
        ]
        wind = [[scales[axis] * extrap[axis][t] for t in range(8)] for axis in range(3)]
        c_at = sub & 3
        spin = []
        for k in range(4):
            value = jnp.zeros((ROWS, 128), F32)
            for c in range(4):
                value = jnp.where(c_at == c, F32(SLOPE[c, (c + k) % 4]), value)
            spin.append(value)
        same = [[pattern(SLOPE[2 * p, 2 * o], SLOPE[2 * p + 1, 2 * o + 1]) for o in range(2)] for p in range(2)]
        cross = [[pattern(SLOPE[2 * p, 2 * o + 1], SLOPE[2 * p + 1, 2 * o]) for o in range(2)] for p in range(2)]
        packed = []
        for comp in range(3):
            ue = extrap[comp]
            flipped = [subs(ue[t], 4) for t in range(8)]
            tiles = []
            for t in range(8):
                a, half = t // 2, t % 2
                along_a = combine(SLOPE[a], [ue[2 * o + half] for o in range(4)])
                along_b = (
                    same[half][0] * ue[2 * a]
                    + cross[half][0] * flipped[2 * a]
                    + same[half][1] * ue[2 * a + 1]
                    + cross[half][1] * flipped[2 * a + 1]
                )
                along_c = spin[0] * ue[t]
                for k in range(1, 4):
                    moved = jnp.where(c_at + k < 4, subs(ue[t], -k), subs(ue[t], 4 - k))
                    along_c = along_c + spin[k] * moved
                advect = wind[0][t] * along_a + wind[1][t] * along_b + wind[2][t] * along_c
                base = (
                    3.0 * level(0, comp, t)
                    - 1.5 * level(1, comp, t)
                    + level(2, comp, t) * F32(1.0 / 3.0)
                )
                tiles.append(base + advect)
            packed.append(swap_groups(tiles, group))

        for piece in range(8):
            flow, slot = places[piece]
            rank = count[flow]

            @pl.when(flow != me)
            def _(flow=flow, slot=slot, rank=rank, piece=piece):
                count[flow] = rank + 1
                row = pl.multiple_of(flow * PEER_ROWS + rank * BLOCK_ROWS, ROWS)
                for comp in range(3):
                    send[pl.ds(row + comp * ROWS, ROWS), :] = packed[comp][piece]
                mark = pl.multiple_of(flow * PEER_ROWS + CAP * BLOCK_ROWS, ROWS)
                old = send[pl.ds(mark, ROWS), :]
                here = (sub == 0) & (lane == CAP * me + rank)
                send[pl.ds(mark, ROWS), :] = jnp.where(here, (slot + 1).astype(F32), old)

            @pl.when(flow == me)
            def _(slot=slot, piece=piece):
                row = pl.multiple_of(slot * BLOCK_ROWS, ROWS)
                for comp in range(3):
                    keep[pl.ds(row + comp * ROWS, ROWS), :] = packed[comp][piece]

        return carry

    lax.fori_loop(0, columns, column, 0)


def at(a, b, c, h):
    return pl.ds((a * 16 + b * 4 + c) * 16 + h * ROWS, ROWS)


def join_radial(line, lane):
    first = line[0] + jnp.where(lane == 0, 0.0, lanes(line[3], 1))
    last = jnp.where(lane == 127, 0.0, lanes(first, -1))
    return [first, line[1], line[2], last]


def join_azim(ref, sub):
    ey = sub & 3
    for a in range(4):
        for c in range(4):
            for h in range(2):
                low = ref[at(a, 0, c, h), :]
                high = ref[at(a, 3, c, h), :]
                ref[at(a, 0, c, h), :] = low + jnp.where(ey == 0, 0.0, subs(high, 1))
                ref[at(a, 3, c, h), :] = high + jnp.where(ey == 3, 0.0, subs(low, -1))


def join_axial(ref, b, c, sub):
    top = sub < 4
    low = [ref[at(0, b, c, h), :] for h in range(2)]
    high = [ref[at(3, b, c, h), :] for h in range(2)]
    low_turned = [subs(x, 4) for x in low]
    high_turned = [subs(x, 4) for x in high]
    new_low = [
        low[0] + jnp.where(top, 0.0, high_turned[0]),
        low[1] + jnp.where(top, high_turned[0], high_turned[1]),
    ]
    new_high = [
        high[0] + jnp.where(top, low_turned[0], low_turned[1]),
        high[1] + jnp.where(top, low_turned[1], 0.0),
    ]
    return new_low, new_high


def lengths(len_axial, len_azim, len_radial, sub):
    slab = lax.axis_index("stream")
    sector = lax.axis_index("azim")
    columns, rows = len_axial.shape[0], len_azim.shape[0]
    x0, y0 = slab * 4, sector * 4
    top = sub < 4
    axial = [jnp.where(top, len_axial[x0 + 2 * h], len_axial[x0 + 2 * h + 1]) for h in range(2)]
    azim = choose(sub & 3, [jnp.full((ROWS, 128), len_azim[y0 + k], F32) for k in range(4)])
    radial = jnp.broadcast_to(len_radial[...], (ROWS, 128))
    before = len_axial[jnp.maximum(x0 - 1, 0)]
    after = len_axial[jnp.minimum(x0 + 4, columns - 1)]
    below = len_azim[lax.rem(y0 + rows - 1, rows)]
    above = len_azim[lax.rem(y0 + 4, rows)]
    return axial, azim, radial, (before, after, below, above)


def load_kernel(
    len_axial, len_azim, len_radial, solid, arrived, keep, pred, part, up, down, blocks, marks, marks_s, sem, sem2
):
    lane, sub = iotas()
    group = lane >> 4
    peers = arrived.shape[0] // PEER_ROWS
    fetch = pltpu.make_async_copy(keep, blocks, sem)
    fetch.start()
    total = None
    for t in range(peers):
        tile = arrived[pl.ds(t * PEER_ROWS + CAP * BLOCK_ROWS, ROWS), :]
        total = tile if total is None else total + tile
    marks[...] = total.astype(jnp.int32)
    scalars = pltpu.make_async_copy(marks, marks_s, sem2)
    scalars.start()
    scalars.wait()
    fetch.wait()

    def place(n, carry):
        label = marks_s[0, n]

        @pl.when(label > 0)
        def _():
            target = pl.multiple_of((label - 1) * BLOCK_ROWS, ROWS)
            source = pl.multiple_of((n // CAP) * PEER_ROWS + (n % CAP) * BLOCK_ROWS, ROWS)
            for comp in range(3):
                blocks[pl.ds(target + comp * ROWS, ROWS), :] = arrived[
                    pl.ds(source + comp * ROWS, ROWS), :
                ]

        return carry

    lax.fori_loop(0, peers * CAP, place, 0)

    def unpack(j, carry):
        for comp in range(3):
            tiles = [
                blocks[pl.ds(pl.multiple_of((j * 8 + g) * BLOCK_ROWS, ROWS) + comp * ROWS, ROWS), :]
                for g in range(8)
            ]
            for t, tile in enumerate(swap_groups(tiles, group)):
                pred[pl.ds(comp * 1024 + 8 * t * 16 + j, ROWS, stride=16), :] = tile
        return carry

    lax.fori_loop(0, 16, unpack, 0)

    axial, azim, radial, _ = lengths(len_axial, len_azim, len_radial, sub)
    inverse = [
        1.0 / (F32(11.0 / 6.0) + F32(DT * PENALTY) * solid[pl.ds(h * ROWS, ROWS), :].astype(F32))
        for h in range(2)
    ]

    def scaled(comp, a, b, c, h):
        spot = pl.ds(comp * 1024 + (a * 16 + b * 4 + c) * 16 + h * ROWS, ROWS)
        value = pred[spot, :] * inverse[h]
        pred[spot, :] = value
        return value

    area = [
        [0.25 * azim * radial for h in range(2)],
        [0.25 * axial[h] * radial for h in range(2)],
        [0.25 * axial[h] * azim for h in range(2)],
    ]
    for h in range(2):
        for b in range(4):
            for c in range(4):
                line = [scaled(0, a, b, c, h) for a in range(4)]
                for a in range(4):
                    part[at(a, b, c, h), :] = area[0][h] * combine(SLOPE[a], line)
        for a in range(4):
            for c in range(4):
                line = [scaled(1, a, b, c, h) for b in range(4)]
                for b in range(4):
                    part[at(a, b, c, h), :] += area[1][h] * combine(SLOPE[b], line)
        for a in range(4):
            for b in range(4):
                line = [scaled(2, a, b, c, h) for c in range(4)]
                line = [
                    float(-WEIGHT[a] * WEIGHT[b] * WEIGHT[c])
                    * (part[at(a, b, c, h), :] + area[2][h] * combine(SLOPE[c], line))
                    for c in range(4)
                ]
                for c, value in enumerate(join_radial(line, lane)):
                    part[at(a, b, c, h), :] = value
    join_azim(part, sub)
    top = sub < 4
    for b in range(4):
        for c in range(4):
            low, high = join_axial(part, b, c, sub)
            for h in range(2):
                part[at(0, b, c, h), :] = low[h]
                part[at(3, b, c, h), :] = high[h]
            inner = [[part[at(a, b, c, h), :] for a in (1, 2)] for h in range(2)]
            spot = pl.ds((b * 4 + c) * ROWS, ROWS)
            normal = combine(STIFF[3], [low[1], *inner[1], high[1]])
            up[spot, :] = jnp.where(top, subs(high[1], 4), normal)
            normal = combine(STIFF[0], [low[0], *inner[0], high[0]])
            down[spot, :] = jnp.where(top, low[0], subs(normal, 4))


def axial_kernel(part, below, above, field, normals, up, down):
    lane, sub = iotas()
    top = sub < 4
    slab = lax.axis_index("stream")
    first = jnp.where(slab == 0, F32(0.0), F32(1.0))
    last = jnp.where(slab == lax.axis_size("stream") - 1, F32(0.0), F32(1.0))
    for b in range(4):
        for c in range(4):
            spot = pl.ds((b * 4 + c) * ROWS, ROWS)
            low = part[at(0, b, c, 0), :]
            high = part[at(3, b, c, 1), :]
            under, over = below[spot, :], above[spot, :]
            normals[spot, :] = jnp.where(
                top,
                subs(under, 4) + float(STIFF[3, 3]) * low,
                over + float(STIFF[0, 0]) * high,
            )
            field[at(0, b, c, 0), :] = low + jnp.where(top, first * under, 0.0)
            field[at(3, b, c, 1), :] = jnp.where(top, high, last * (high + subs(over, 4)))
            field[at(0, b, c, 1), :] = part[at(0, b, c, 1), :]
            field[at(3, b, c, 0), :] = part[at(3, b, c, 0), :]
            for a in (1, 2):
                for h in range(2):
                    field[at(a, b, c, h), :] = part[at(a, b, c, h), :]
    ey = sub & 3
    for a in range(4):
        for c in range(4):
            spot = pl.ds((a * 4 + c) * ROWS, ROWS)
            line = [[field[at(a, b, c, h), :] for b in range(4)] for h in range(2)]
            normal = [combine(STIFF[3], line[h]) for h in range(2)]
            up[spot, :] = choose(
                ey, [subs(normal[1], -3), subs(normal[0], -2), subs(line[1][3], -1), line[0][3]]
            )
            normal = [combine(STIFF[0], line[h]) for h in range(2)]
            down[spot, :] = choose(
                ey, [line[0][0], subs(line[1][0], 1), subs(normal[0], 2), subs(normal[1], 3)]
            )
    spot = pl.ds(16 * ROWS, ROWS)
    edge = [normals[pl.ds((12 + c) * ROWS, ROWS), :] for c in range(4)]
    up[spot, :] = choose(ey, [subs(edge[3], -3), subs(edge[2], -2), subs(edge[1], -1), edge[0]])
    edge = [normals[pl.ds(c * ROWS, ROWS), :] for c in range(4)]
    down[spot, :] = choose(ey, [edge[0], subs(edge[1], 1), subs(edge[2], 2), subs(edge[3], 3)])


def image_kernel(
    len_axial, len_azim, len_radial, part, normals_in, below, above, field, image, sums, normals, sides
):
    lane, sub = iotas()
    top = sub < 4
    ey = sub & 3
    slab = lax.axis_index("stream")
    first = jnp.where(slab == 0, F32(0.0), F32(1.0))
    last = jnp.where(slab == lax.axis_size("stream") - 1, F32(0.0), F32(1.0))
    for a in range(4):
        for c in range(4):
            spot = pl.ds((a * 4 + c) * ROWS, ROWS)
            under, over = below[spot, :], above[spot, :]
            under_face = [subs(under, -3), subs(under, -2)]
            under_normal = [subs(under, -1), under]
            over_face = [subs(over, 3), subs(over, 2)]
            over_normal = [subs(over, 1), over]
            for h in range(2):
                low = part[at(a, 0, c, h), :]
                high = part[at(a, 3, c, h), :]
                sides[pl.ds(((a * 4 + c) * 2 + h) * ROWS, ROWS), :] = jnp.where(
                    ey == 0,
                    under_normal[h] + float(STIFF[3, 3]) * low,
                    over_normal[h] + float(STIFF[0, 0]) * high,
                )
                field[at(a, 0, c, h), :] = low + jnp.where(ey == 0, under_face[h], 0.0)
                field[at(a, 3, c, h), :] = high + jnp.where(ey == 3, over_face[h], 0.0)
                for b in (1, 2):
                    field[at(a, b, c, h), :] = part[at(a, b, c, h), :]
    under, over = below[pl.ds(16 * ROWS, ROWS), :], above[pl.ds(16 * ROWS, ROWS), :]
    for c in range(4):
        spot = pl.ds(c * ROWS, ROWS)
        normals[spot, :] = normals_in[spot, :] + jnp.where(ey == 0, subs(under, c - 3), 0.0)
        spot = pl.ds((12 + c) * ROWS, ROWS)
        normals[spot, :] = normals_in[spot, :] + jnp.where(ey == 3, subs(over, 3 - c), 0.0)
        for b in (1, 2):
            spot = pl.ds((b * 4 + c) * ROWS, ROWS)
            normals[spot, :] = normals_in[spot, :]

    axial, azim, radial, (before, after, beneath, beyond) = lengths(
        len_axial, len_azim, len_radial, sub
    )
    zero = jnp.zeros((ROWS, 128), F32)
    rx = [2.0 / axial[h] for h in range(2)]
    ry = 2.0 / azim
    rz = 2.0 / radial
    qz = 0.5 * radial
    qx = [[0.5 * axial[h] for a in range(4)] for h in range(2)]
    before_v, after_v = jnp.full((ROWS, 128), before, F32), jnp.full((ROWS, 128), after, F32)
    beneath_v, beyond_v = jnp.full((ROWS, 128), beneath, F32), jnp.full((ROWS, 128), beyond, F32)
    own_x = [qx[h][0] for h in range(2)]
    qx[0][0] = own_x[0] + jnp.where(top, first * 0.5 * before_v, 0.0)
    qx[1][3] = own_x[1] + jnp.where(top, 0.0, last * 0.5 * after_v)
    ghost_x = [jnp.where(top, first * 2.0 / before_v, 0.0), jnp.where(top, 0.0, last * 2.0 / after_v)]
    own_y = 0.5 * azim
    qy = [
        own_y + jnp.where(ey == 0, 0.5 * beneath_v, 0.0),
        own_y,
        own_y,
        own_y + jnp.where(ey == 3, 0.5 * beyond_v, 0.0),
    ]
    ghost_y = [jnp.where(ey == 0, 2.0 / beneath_v, 0.0), zero, zero, jnp.where(ey == 3, 2.0 / beyond_v, 0.0)]

    for h in range(2):
        factor = [rx[h] * qz * qy[b] for b in range(4)]
        extra = [ghost_x[h] * qz * qy[b] for b in range(4)]
        edge_a = 0 if h == 0 else 3
        for b in range(4):
            for c in range(4):
                line = [field[at(a, b, c, h), :] for a in range(4)]
                for a in range(4):
                    value = factor[b] * combine(STIFF[a], line)
                    if a == edge_a:
                        value = value + extra[b] * normals[pl.ds((b * 4 + c) * ROWS, ROWS), :]
                    image[at(a, b, c, h), :] = float(WEIGHT[b] * WEIGHT[c]) * value
        for a in range(4):
            factor_a = ry * qz * qx[h][a]
            extra_a = [ghost_y[b] * qz * qx[h][a] for b in range(4)]
            for c in range(4):
                line = [field[at(a, b, c, h), :] for b in range(4)]
                side = sides[pl.ds(((a * 4 + c) * 2 + h) * ROWS, ROWS), :]
                for b in range(4):
                    value = factor_a * combine(STIFF[b], line)
                    if b in (0, 3):
                        value = value + extra_a[b] * side
                    image[at(a, b, c, h), :] += float(WEIGHT[a] * WEIGHT[c]) * value
        for a in range(4):
            for b in range(4):
                factor_ab = (float(WEIGHT[a] * WEIGHT[b]) * rz) * qx[h][a] * qy[b]
                line = [field[at(a, b, c, h), :] for c in range(4)]
                line = [
                    image[at(a, b, c, h), :] + factor_ab * combine(STIFF[c], line)
                    for c in range(4)
                ]
                for c, value in enumerate(join_radial(line, lane)):
                    image[at(a, b, c, h), :] = value
    join_azim(image, sub)
    outlet = jnp.where(top, 1.0, last)
    for b in range(4):
        for c in range(4):
            low, high = join_axial(image, b, c, sub)
            high[1] = high[1] * outlet
            for h in range(2):
                image[at(0, b, c, h), :] = low[h]
                image[at(3, b, c, h), :] = high[h]

    load_load = load_image = image_image = zero
    for h in range(2):
        for a in range(3):
            for b in range(3):
                for c in range(3):
                    one, two = field[at(a, b, c, h), :], image[at(a, b, c, h), :]
                    load_load = load_load + one * one
                    load_image = load_image + one * two
                    image_image = image_image + two * two
    energy = zero
    for h in range(2):
        along = [zero, zero, zero]
        for m in range(4):
            for n in range(4):
                weight = float(WEIGHT[m] * WEIGHT[n])
                lines = (
                    [image[at(k, m, n, h), :] for k in range(4)],
                    [image[at(m, k, n, h), :] for k in range(4)],
                    [image[at(m, n, k, h), :] for k in range(4)],
                )
                for axis, line in enumerate(lines):
                    dot = None
                    for k in range(4):
                        term = line[k] * combine(STIFF[k], line)
                        dot = term if dot is None else dot + term
                    along[axis] = along[axis] + weight * dot
        energy = (
            energy
            + rx[h] * own_y * qz * along[0]
            + ry * own_x[h] * qz * along[1]
            + rz * own_x[h] * own_y * along[2]
        )
    row = zero
    for k, value in enumerate((load_load, load_image, image_image, energy)):
        value = jnp.sum(jnp.sum(value, axis=0, keepdims=True), axis=1, keepdims=True)
        row = jnp.where(lane == k, jnp.broadcast_to(value, (ROWS, 128)), row)
    for k in range(sums.shape[0] // ROWS):
        sums[pl.ds(k * ROWS, ROWS), :] = row


def final_kernel(len_axial, len_azim, len_radial, sums, field, image, pred, velocity, pressure):
    lane, sub = iotas()
    total = sums[pl.ds(0, ROWS), :]
    for k in range(1, sums.shape[0] // ROWS):
        total = total + sums[pl.ds(k * ROWS, ROWS), :]
    total = jnp.broadcast_to(jnp.sum(total, axis=0, keepdims=True), (ROWS, 128))
    s0, s1, s2, s3 = (
        jnp.broadcast_to(
            jnp.sum(jnp.where(lane == k, total, 0.0), axis=1, keepdims=True), (ROWS, 128)
        )
        for k in range(4)
    )
    alpha = s0 / s1
    ratio = s2 / s1
    grown = alpha * ratio
    energy = alpha * (s3 - s2 * ratio)
    second = s0 * (grown - 1.0) / (alpha * energy)
    of_load = alpha + second * grown
    of_image = -(second * alpha)

    axial, azim, radial, _ = lengths(len_axial, len_azim, len_radial, sub)
    for h in range(2):
        for a in range(4):
            for b in range(4):
                for c in range(4):
                    spot = at(a, b, c, h)
                    pressure[spot, :] = of_load * field[spot, :] + of_image * image[spot, :]
    for h in range(2):
        scales = (2.0 / axial[h], 2.0 / azim, 2.0 / radial)
        for m in range(4):
            for n in range(4):
                lines = (
                    [(k, m, n) for k in range(4)],
                    [(m, k, n) for k in range(4)],
                    [(m, n, k) for k in range(4)],
                )
                for axis, line in enumerate(lines):
                    values = [pressure[at(*node, h), :] for node in line]
                    for k, (a, b, c) in enumerate(line):
                        spot = pl.ds(axis * 1024 + (a * 16 + b * 4 + c) * 16 + h * ROWS, ROWS)
                        velocity[spot, :] = pred[spot, :] - scales[axis] * combine(
                            SLOPE[k], values
                        )


SMEM = pl.BlockSpec(memory_space=pltpu.SMEM)
VMEM = pl.BlockSpec(memory_space=pltpu.VMEM)
ANY = pl.BlockSpec(memory_space=pl.ANY)


def array(rows, kind=F32):
    return jax.ShapeDtypeStruct((rows, 128), kind)


def call(kernel, ins, outs, scratch, name):
    return pl.pallas_call(
        kernel,
        out_shape=outs,
        in_specs=ins,
        out_specs=[VMEM] * len(outs),
        scratch_shapes=scratch,
        compiler_params=pltpu.CompilerParams(vmem_limit_bytes=VMEM_LIMIT),
        name=name,
    )


def around(axis, value, shift):
    count = lax.axis_size(axis)
    return lax.ppermute(value, axis, [(i, (i + shift) % count) for i in range(count)])


def body(history, block_ids, len_axial, len_azim, len_radial, solid):
    slabs, sectors = lax.axis_size("stream"), lax.axis_size("azim")
    radial = len_radial.reshape(1, 128)
    geometry = (len_axial, len_azim, radial)
    geometry_specs = [SMEM, SMEM, VMEM]
    steps = 4
    hist = history.reshape(576, history.shape[3])
    send, keep = pl.pallas_call(
        pack_kernel,
        grid=(steps,),
        out_shape=[array(slabs * PEER_ROWS), array(128 * BLOCK_ROWS)],
        in_specs=[
            SMEM,
            SMEM,
            SMEM,
            pl.BlockSpec((1, 128), lambda i: (0, 0)),
            pl.BlockSpec((576, hist.shape[1] // steps), lambda i: (0, i)),
        ],
        out_specs=[
            pl.BlockSpec((slabs * PEER_ROWS, 128), lambda i: (0, 0)),
            pl.BlockSpec((128 * BLOCK_ROWS, 128), lambda i: (0, 0)),
        ],
        scratch_shapes=[pltpu.SMEM((slabs,), jnp.int32), pltpu.VMEM((ROWS, 128), F32)],
        compiler_params=pltpu.CompilerParams(
            vmem_limit_bytes=VMEM_LIMIT, dimension_semantics=("arbitrary",)
        ),
        name="pack",
    )(block_ids, len_axial, len_azim, radial, hist)
    arrived = lax.all_to_all(
        send.reshape(slabs, PEER_ROWS, 128), "stream", split_axis=0, concat_axis=0, tiled=True
    ).reshape(slabs * PEER_ROWS, 128)
    pred, part, up, down = call(
        load_kernel,
        geometry_specs + [VMEM, VMEM, ANY],
        [array(3 * 1024), array(1024), array(128), array(128)],
        [
            pltpu.VMEM((128 * BLOCK_ROWS, 128), F32),
            pltpu.VMEM((ROWS, 128), jnp.int32),
            pltpu.SMEM((ROWS, 128), jnp.int32),
            pltpu.SemaphoreType.DMA(()),
            pltpu.SemaphoreType.DMA(()),
        ],
        "load",
    )(*geometry, solid.reshape(16, 128), arrived, keep)
    below, above = around("stream", up, 1), around("stream", down, -1)
    part, normals, up, down = call(
        axial_kernel,
        [VMEM] * 3,
        [array(1024), array(128), array(136), array(136)],
        [],
        "axial_faces",
    )(part, below, above)
    below, above = around("azim", up, 1), around("azim", down, -1)
    field, image, sums = call(
        image_kernel,
        geometry_specs + [VMEM] * 4,
        [array(1024), array(1024), array(slabs * sectors)],
        [pltpu.VMEM((128, 128), F32), pltpu.VMEM((256, 128), F32)],
        "image",
    )(*geometry, part, normals, below, above)
    sums = lax.all_to_all(
        sums.reshape(slabs * sectors, 1, 128),
        ("stream", "azim"),
        split_axis=0,
        concat_axis=0,
        tiled=True,
    ).reshape(slabs * sectors, 128)
    velocity, pressure = call(
        final_kernel,
        geometry_specs + [VMEM] * 4,
        [array(3 * 1024), array(1024)],
        [],
        "velocity",
    )(*geometry, sums, field, image, pred)
    return velocity.reshape(3, 4, 4, 4, 4, 4, 128), pressure.reshape(4, 4, 4, 4, 4, 128)


def solution(mesh):
    in_specs = (
        P(None, None, None, ("stream", "azim")),
        P(("stream", "azim")),
        P(),
        P(),
        P(),
        P("stream", "azim", None),
    )
    out_specs = (
        P(None, None, None, None, "stream", "azim", None),
        P(None, None, None, "stream", "azim", None),
    )
    return jax.shard_map(body, mesh=mesh, in_specs=in_specs, out_specs=out_specs, check_vma=False)
```

time: 536 us -> 79.8 us (0.15); the launches traced: 528 us -> 79.5 us
  local copies, waits for them, and re-layouts: 188 us -> 4.97 us
  blocking collectives: 201 us -> 46.3 us
  matrix products: 43.3 us -> 0 us
  other arithmetic: 35.3 us -> 0 us
  starting transfers between devices: 31.9 us -> 3.35 us
  Pallas kernels: 0 us -> 18.8 us
  waiting for transfers between devices: 22.1 us -> 5.38 us
    psum x3 -> x0, blocking collectives: 201 us -> none  [the longest x2 133 us: squares(): return lax.psum(owned_inner(field, field), ('stream', 'azim'))]
    all_to_all x0 -> x2, blocking collectives: none -> 46.3 us  [the longest x1 25.3 us: body(): lax.all_to_all(send.reshape(slabs, PEER_ROWS, 128), 'stream', split_axis=...]
    dot_general x21 -> x0, matrix products: 43.3 us -> none  [along(): return jnp.einsum(form, slope, field, precision=HIGH)]
    add x4 -> x0, local copies, waits for them, and re-layouts: 39.7 us -> none  [the longest x2 19.8 us: predictor(): extrap = 3.0 * newest - 3.0 * middle + oldest]
    scatter x3 -> x0, local copies, waits for them, and re-layouts: 39.1 us -> none  [the longest x1 25 us: body(): result = result.at[:, :, keep_at].set(blocks)]
    unnamed x78 -> x18, local copies, waits for them, and re-layouts: 28.1 us -> 4.97 us
    pallas_call x0 -> x5, Pallas kernels: none -> 18.8 us  [the longest x1 8.27 us: body(): pl.pallas_call(pack_kernel, grid=(steps,), out_shape=[array(slabs * PEER_...]
    slice x14 -> x0, local copies, waits for them, and re-layouts: 17.6 us -> none  [the longest x4 16.5 us: predictor(): extrap[axis_pick] * (scales[axis_pick] * along(extrap, axis_pick, False))]
  transfers between devices with their start and end apart: 14 -> 4, of which waited for: 10 -> 3; matrix products, arithmetic and copies ran while one was open for 16% -> 0% of each run, Pallas kernels for 0% -> 0%
where the time goes in v1:
time: 79.8 us; the launch traced here: 79.5 us
  blocking collectives  46.3 us (58%)
  Pallas kernels  18.8 us (24%)
  waiting for transfers between devices  5.38 us (7%)
  local copies, waits for them, and re-layouts  4.97 us (6%)
  starting transfers between devices  3.35 us (4%)
    all_to_all x1, blocking collectives, body(): lax.all_to_all(send.reshape(slabs, PEER_ROWS, 128), 'stream', split_axis=...  25.3 us
    all_to_all x1, blocking collectives, body(): lax.all_to_all(sums.reshape(slabs * sectors, 1, 128), ('stream', 'azim'),...  21 us
    pallas_call x1, Pallas kernels, body(): pl.pallas_call(pack_kernel, grid=(steps,), out_shape=[array(slabs * PEER_...  8.27 us
    pallas_call x1, Pallas kernels, body(): call(load_kernel, geometry_specs + [VMEM, VMEM, ANY], [array(3 * 1024), a...  6.29 us
    ppermute x4, waiting for transfers between devices, around(): lax.ppermute(value, axis, [(i, (i + shift) % count) for i in range(count)])  5.38 us
    unnamed x18, local copies, waits for them, and re-layouts  4.97 us
    ppermute x4, starting transfers between devices, around(): lax.ppermute(value, axis, [(i, (i + shift) % count) for i in range(count)])  3.35 us
    pallas_call x1, Pallas kernels, body(): call(final_kernel, geometry_specs + [VMEM] * 4, [array(3 * 1024), array(1...  2.3 us
  transfers between devices with their start and end apart: 4, of which 3 were waited for; matrix products, arithmetic and copies ran while one was open for 0% of the time, Pallas kernels for 0%

profile of v1, /device:TPU:1, one launch (start us, length us, event | category | flops | bytes accessed | tf_op | source)
XLA Modules:
  0.0 79.5 jit_solution(2253446971685683209)
XLA Ops:
  0.6 0.0 copy-start
  0.6 2.3 %copy-done = f32[3,3,64,2048]{3,2,1,0:T(8,128)S(1)} copy-done((f32[3,3,64,2048]{3,2,1,0:T(8,128)S(1)}, f32[3,3,64,2048]{3,2,1,0:T(8,128)}, u32[]{:S(2)}) %copy-start) | copy-done | bytes 4718616
  3.0 0.0 copy-start.2
  3.0 0.7 copy-done.2
  3.6 0.0 copy-start.4
  3.6 0.7 copy-done.4
  4.3 0.0 copy-start.6
  4.3 0.7 copy-done.6
  4.9 0.0 copy-start.8
  4.9 0.7 copy-done.8
  5.6 8.3 %pack.1 = (f32[1792,128]{1,0:T(8,128)S(1)}, f32[3072,128]{1,0:T(8,128)S(1)}) custom-call(s32[128]{0:T(128)S(1)} %copy-done.8, f32[128]{0:T(128)S(1)} %copy-done.2, f32[16]{0:T(128)S(1)} %copy-done.4, f32[1,128]{1,0:T(1,128)S(1)} %bitcast.17, f32[576,2048]{1,0:T(8,128)S(1)} %bitcast.11), custom_call_target="tpu_custom_call" | custom-call | tf_op jit(solution)/shard_map/pack/pallas_call | solution.py:629
  13.9 0.0 copy-start.1
  13.9 0.0 copy-start.3
  13.9 0.0 copy-start.5
  13.9 0.0 copy-start.7
  13.9 25.3 %all_to_all.10 = f32[32,56,128]{2,1,0:T(8,128)S(1)} all-to-all(f32[32,56,128]{2,1,0:T(8,128)S(1)} %bitcast.13), channel_id=1, replica_groups=mesh['stream'=32,'azim'=4] {'stream'}, dimensions={0} | all-to-all | bytes 1835008 | tf_op jit(solution)/shard_map/all_to_all | solution.py:650
  39.2 0.0 copy-done.1
  39.2 0.0 copy-done.3
  39.2 0.0 copy-done.5
  39.2 0.0 copy-done.7
  39.2 6.3 %load.1 = (f32[3072,128]{1,0:T(8,128)S(1)}, f32[1024,128]{1,0:T(8,128)S(1)}, f32[128,128]{1,0:T(8,128)S(1)}, f32[128,128]{1,0:T(8,128)S(1)}) custom-call(f32[128]{0:T(128)S(1)} %copy-done.3, f32[16]{0:T(128)S(1)} %copy-done.5, f32[1,128]{1,0:T(1,128)S(1)} %bitcast.18, s32[16,128]{1,0:T(8,128)S(1)} %bitcast.16, f32[1792,128]{1,0:T(8,128)S(1)} %bitcast.12, ...), custom_call_target="tpu_custom_call" | custom-call | tf_op jit(solution)/shard_map/load/pallas_call | solution.py:653
  45.5 0.6 collective-permute-start
  46.1 0.0 collective-permute-start.1
  46.1 1.3 %collective-permute-done.below = f32[128,128]{1,0:T(8,128)S(1)} collective-permute-done((f32[128,128]{1,0:T(8,128)S(1)}, f32[128,128]{1,0:T(8,128)S(1)}, u32[]{:S(2)}, u32[]{:S(2)}) %collective-permute-start) | collective-permute-done | bytes 65568 | tf_op jit(solution)/shard_map/ppermute | solution.py:619
  47.5 2.4 %collective-permute-done.1.above = f32[128,128]{1,0:T(8,128)S(1)} collective-permute-done((f32[128,128]{1,0:T(8,128)S(1)}, f32[128,128]{1,0:T(8,128)S(1)}, u32[]{:S(2)}, u32[]{:S(2)}) %collective-permute-start.1) | collective-permute-done | bytes 65568 | tf_op jit(solution)/shard_map/ppermute | solution.py:619
  49.8 0.1 axial_faces.1
  50.0 1.2 %collective-permute-start.2 = (f32[136,128]{1,0:T(8,128)S(1)}, f32[136,128]{1,0:T(8,128)S(1)}, u32[]{:S(2)}, u32[]{:S(2)}) collective-permute-start(f32[136,128]{1,0:T(8,128)S(1)} %get-tuple-element.24), channel_id=1, source_target_pairs={{0,1},{1,2},{2,3},{3,0},{4,5},{5,6},{6,7},{7,4},{8,9},{9,10},{10,1... | collective-permute-start | bytes 208904 | tf_op jit(solution)/shard_map/ppermute | solution.py:619
  51.2 1.5 %collective-permute-start.3 = (f32[136,128]{1,0:T(8,128)S(1)}, f32[136,128]{1,0:T(8,128)S(1)}, u32[]{:S(2)}, u32[]{:S(2)}) collective-permute-start(f32[136,128]{1,0:T(8,128)S(1)} %get-tuple-element.25), channel_id=1, source_target_pairs={{0,3},{1,0},{2,1},{3,2},{4,7},{5,4},{6,5},{7,6},{8,11},{9,8},{10,9... | collective-permute-start | bytes 208904 | tf_op jit(solution)/shard_map/ppermute | solution.py:619
  52.7 1.7 %collective-permute-done.2.below = f32[136,128]{1,0:T(8,128)S(1)} collective-permute-done((f32[136,128]{1,0:T(8,128)S(1)}, f32[136,128]{1,0:T(8,128)S(1)}, u32[]{:S(2)}, u32[]{:S(2)}) %collective-permute-start.2) | collective-permute-done | bytes 69664 | tf_op jit(solution)/shard_map/ppermute | solution.py:619
  54.4 0.0 collective-permute-done.3.above
  54.4 1.8 %image.1 = (f32[1024,128]{1,0:T(8,128)S(1)}, f32[1024,128]{1,0:T(8,128)S(1)}, f32[128,128]{1,0:T(8,128)S(1)}) custom-call(f32[128]{0:T(128)S(1)} %copy-done.3, f32[16]{0:T(128)S(1)} %copy-done.5, f32[1,128]{1,0:T(1,128)S(1)} %bitcast.19, f32[1024,128]{1,0:T(8,128)S(1)} %get-tuple-element.22.part, f32[128,128]{1,0:T(8,128)S(1)} %get-tuple-element.23.normals_in, ...), custom_call_target="tpu_custom_call" | custom-call | tf_op jit(solution)/shard_map/image/pallas_call | solution.py:675
  56.2 21.0 %all_to_all.11 = f32[128,1,128]{2,1,0:T(1,128)S(1)} all-to-all(f32[128,1,128]{2,1,0:T(1,128)S(1)} %bitcast.15), channel_id=1, replica_groups=mesh['stream'=32,'azim'=4] {'stream','azim'}, dimensions={0} | all-to-all | bytes 131072 | tf_op jit(solution)/shard_map/all_to_all | solution.py:682
  77.2 2.3 %velocity.1 = (f32[3072,128]{1,0:T(8,128)}, f32[1024,128]{1,0:T(8,128)}) custom-call(f32[128]{0:T(128)S(1)} %copy-done.3, f32[16]{0:T(128)S(1)} %copy-done.5, f32[1,128]{1,0:T(1,128)S(1)} %bitcast.20, f32[128,128]{1,0:T(8,128)S(1)} %bitcast.14, f32[1024,128]{1,0:T(8,128)S(1)} %get-tuple-element.27.field, f32[1024,128]{1,0:T(8,128)S(1)} %get-tuple-element.28.image, ...), custom_call_target="tpu_custom_call" | custom-call | tf_op jit(solution)/shard_map/velocity/pallas_call | solution.py:689
Async XLA Ops:
  0.6 2.3 %copy-start = (f32[3,3,64,2048]{3,2,1,0:T(8,128)S(1)}, f32[3,3,64,2048]{3,2,1,0:T(8,128)}, u32[]{:S(2)}) copy-start(f32[3,3,64,2048]{3,2,1,0:T(8,128)} %param.6) | copy-start | bytes 14155780
  3.0 0.7 copy-start.2
  3.6 0.7 copy-start.4
  4.3 0.7 copy-start.6
  4.9 0.7 copy-start.8
  13.9 25.4 %copy-start.1 = (s32[4,4,128]{2,1,0:T(4,128)S(1)}, s32[4,4,128]{2,1,0:T(4,128)}, u32[]{:S(2)}) copy-start(s32[4,4,128]{2,1,0:T(4,128)} %param.11) | copy-start | bytes 24580
  13.9 25.3 %copy-start.3 = (f32[128]{0:T(128)S(1)}, f32[128]{0:T(128)}, u32[]{:S(2)}) copy-start(f32[128]{0:T(128)} %len_axial.7) | copy-start | bytes 1540
  13.9 25.3 %copy-start.5 = (f32[16]{0:T(128)S(1)}, f32[16]{0:T(128)}, u32[]{:S(2)}) copy-start(f32[16]{0:T(128)} %len_azim.7) | copy-start | bytes 196
  13.9 25.3 %copy-start.7 = (f32[128]{0:T(128)S(1)}, f32[128]{0:T(128)}, u32[]{:S(2)}) copy-start(f32[128]{0:T(128)} %param.10) | copy-start | bytes 1540
  45.5 1.9 %collective-permute-start = (f32[128,128]{1,0:T(8,128)S(1)}, f32[128,128]{1,0:T(8,128)S(1)}, u32[]{:S(2)}, u32[]{:S(2)}) collective-permute-start(f32[128,128]{1,0:T(8,128)S(1)} %get-tuple-element.20), channel_id=1, source_target_pairs={{0,4},{4,8},{8,12},{12,16},{16,20},{20,24},{24,28},{28,32},{32,36}... | collective-permute-start | bytes 196616 | tf_op jit(solution)/shard_map/ppermute | solution.py:619
  46.1 3.7 %collective-permute-start.1 = (f32[128,128]{1,0:T(8,128)S(1)}, f32[128,128]{1,0:T(8,128)S(1)}, u32[]{:S(2)}, u32[]{:S(2)}) collective-permute-start(f32[128,128]{1,0:T(8,128)S(1)} %get-tuple-element.21), channel_id=1, source_target_pairs={{0,124},{4,0},{8,4},{12,8},{16,12},{20,16},{24,20},{28,24},{32,28}... | collective-permute-start | bytes 196616 | tf_op jit(solution)/shard_map/ppermute | solution.py:619
  50.0 4.4 %collective-permute-start.2 = (f32[136,128]{1,0:T(8,128)S(1)}, f32[136,128]{1,0:T(8,128)S(1)}, u32[]{:S(2)}, u32[]{:S(2)}) collective-permute-start(f32[136,128]{1,0:T(8,128)S(1)} %get-tuple-element.24), channel_id=1, source_target_pairs={{0,1},{1,2},{2,3},{3,0},{4,5},{5,6},{6,7},{7,4},{8,9},{9,10},{10,1... | collective-permute-start | bytes 208904 | tf_op jit(solution)/shard_map/ppermute | solution.py:619
  51.2 3.2 %collective-permute-start.3 = (f32[136,128]{1,0:T(8,128)S(1)}, f32[136,128]{1,0:T(8,128)S(1)}, u32[]{:S(2)}, u32[]{:S(2)}) collective-permute-start(f32[136,128]{1,0:T(8,128)S(1)} %get-tuple-element.25), channel_id=1, source_target_pairs={{0,3},{1,0},{2,1},{3,2},{4,7},{5,4},{6,5},{7,6},{8,11},{9,8},{10,9... | collective-permute-start | bytes 208904 | tf_op jit(solution)/shard_map/ppermute | solution.py:619

commit v2 on v1

--- a/solution.py
+++ b/solution.py
@@ -13,6 +13,7 @@
 DT = 0.01
 PENALTY = 100.0
 VMEM_LIMIT = 40 * 1024 * 1024
+PACK_LIMIT = 60 * 1024 * 1024
 F32 = jnp.float32
 
 
@@ -58,15 +59,31 @@
     return pltpu.roll(x, shift, 0) if shift else x
 
 
-def combine(coefs, values):
+def combine(coefs, values, factor=1.0):
     total = None
     for coef, value in zip(coefs, values):
-        coef = float(coef)
-        if coef == 0.0:
-            continue
+        coef = factor * float(coef)
         term = coef * value
         total = term if total is None else total + term
     return total
+
+
+def halves(line):
+    return (line[0] + line[3], line[1] + line[2]), (line[0] - line[3], line[1] - line[2])
+
+
+def slope_along(line):
+    even, odd = halves(line)
+    first = [combine(SLOPE[i, :2] - SLOPE[i, :1:-1], odd, 0.5) for i in range(2)]
+    second = [combine(SLOPE[i, :2] + SLOPE[i, :1:-1], even, 0.5) for i in range(2)]
+    return [first[0] + second[0], first[1] + second[1], first[1] - second[1], first[0] - second[0]]
+
+
+def stiff_along(line):
+    even, odd = halves(line)
+    first = [combine(STIFF[i, :2] + STIFF[i, :1:-1], even, 0.5) for i in range(2)]
+    second = [combine(STIFF[i, :2] - STIFF[i, :1:-1], odd, 0.5) for i in range(2)]
+    return [first[0] + second[0], first[1] + second[1], first[1] - second[1], first[0] - second[0]]
 
 
 def choose(key, values):
@@ -77,38 +94,66 @@
 
 
 def swap_groups(tiles, group):
-    turned = [lanes(tile, 16 * t) for t, tile in enumerate(tiles)]
-    result = []
-    for g in range(8):
-        mixed = choose((group - g) & 7, turned)
-        result.append(lanes(mixed, -16 * g))
-    return result
-
-
-def pack_kernel(ids, len_axial, len_azim, len_radial, hist, send, keep, count, table):
+    mixed = [lanes(tile, 16 * t) for t, tile in enumerate(tiles)]
+    for bit in (1, 2, 4):
+        odd = (group & bit) != 0
+        mixed = [jnp.where(odd, mixed[(t + bit) & 7], mixed[t]) for t in range(8)]
+    return [lanes(mixed[-g & 7], -16 * g) for g in range(8)]
+
+
+CHUNKS = 4
+
+
+def pack_kernel(
+    ids_h, axial_h, azim_h, radial_h, hist_h, send_h, keep_h,
+    hist, send, keep, ids, len_axial, len_azim, len_radial, count, labels, table,
+    hist_sem, keep_sem, small_sem,
+):
     sectors = lax.axis_size("azim")
+    peers = lax.axis_size("stream")
     me = lax.axis_index("stream")
-    step = pl.program_id(0)
-    columns = hist.shape[1] // 128
+    width = hist.shape[1] // CHUNKS
+    columns = width // 128
+
+    def chunk(n):
+        span = pl.ds(pl.multiple_of(n * width, width), width)
+        return pltpu.make_async_copy(hist_h.at[:, span], hist.at[:, span], hist_sem.at[n])
+
+    def kept(n):
+        rows = keep.shape[0] // CHUNKS
+        span = pl.ds(pl.multiple_of(n * rows, rows), rows)
+        return pltpu.make_async_copy(keep.at[span, :], keep_h.at[span, :], keep_sem.at[n])
+
+    small = [
+        pltpu.make_async_copy(source, target, small_sem.at[n])
+        for n, (source, target) in enumerate(
+            ((ids_h, ids), (axial_h, len_axial), (azim_h, len_azim), (radial_h, len_radial))
+        )
+    ]
+    for copy in small:
+        copy.start()
+    for n in range(CHUNKS):
+        chunk(n).start()
     lane, sub = iotas()
     group = lane >> 4
-
-    @pl.when(step == 0)
-    def _():
-        for t in range(send.shape[0] // PEER_ROWS):
-            count[t] = 0
-            send[pl.ds(t * PEER_ROWS + CAP * BLOCK_ROWS, ROWS), :] = jnp.zeros((ROWS, 128), F32)
-        whole = jnp.broadcast_to(len_radial[...], (ROWS, 128))
-        rows = choose(sub, [lanes(whole, -16 * z) for z in range(8)])
-        rows = jnp.where(group == 0, rows, 0.0)
-        for shift in (16, 32, 64):
-            rows = rows + lanes(rows, shift)
-        table[...] = rows
+    c_at = sub & 3
+    for t in range(peers):
+        count[t] = 0
+    for n in range(CAP * peers):
+        labels[n] = 0
+    for copy in small:
+        copy.wait()
+    whole = jnp.broadcast_to(len_radial[...], (ROWS, 128))
+    rows = choose(sub, [lanes(whole, -16 * z) for z in range(8)])
+    rows = jnp.where(group == 0, rows, 0.0)
+    for shift in (16, 32, 64):
+        rows = rows + lanes(rows, shift)
+    table[...] = rows
 
     def pattern(low, high):
         return jnp.where(sub < 4, F32(low), F32(high))
 
-    def column(at, carry):
+    def column(at):
         offset = pl.multiple_of(at * 128, 128)
 
         def level(which, comp, t):
@@ -117,13 +162,18 @@
         places = []
         axial = azim = radial = None
         for piece in range(8):
-            p = (step * columns + at) * 8 + piece
-            ident = ids[p]
+            ident = ids[at * 8 + piece]
             owner = ident >> 7
             slot = ident & 127
             flow = owner // sectors
             sector = owner - flow * sectors
-            places.append((flow, slot))
+            moving = flow != me
+            rank = jnp.where(moving, count[flow], 0)
+            count[flow] = rank + 1
+            labels[jnp.where(moving, flow * CAP + rank, CAP * peers)] = slot + 1
+            places.append(
+                (flow * PEER_ROWS + rank * BLOCK_ROWS, (at * 8 + piece) * BLOCK_ROWS)
+            )
             one_axial = len_axial[flow * 4 + (slot >> 5)]
             one_azim = len_azim[sector * 4 + ((slot >> 3) & 3)]
             one_radial = table[pl.ds(slot & 7, 1), :]
@@ -138,11 +188,10 @@
         scales = [(-2.0 * DT) / length for length in (axial, azim, radial)]
 
         extrap = [
-            [3.0 * level(0, comp, t) - 3.0 * level(1, comp, t) + level(2, comp, t) for t in range(8)]
+            [3.0 * (level(0, comp, t) - level(1, comp, t)) + level(2, comp, t) for t in range(8)]
             for comp in range(3)
         ]
         wind = [[scales[axis] * extrap[axis][t] for t in range(8)] for axis in range(3)]
-        c_at = sub & 3
         spin = []
         for k in range(4):
             value = jnp.zeros((ROWS, 128), F32)
@@ -151,14 +200,16 @@
             spin.append(value)
         same = [[pattern(SLOPE[2 * p, 2 * o], SLOPE[2 * p + 1, 2 * o + 1]) for o in range(2)] for p in range(2)]
         cross = [[pattern(SLOPE[2 * p, 2 * o + 1], SLOPE[2 * p + 1, 2 * o]) for o in range(2)] for p in range(2)]
-        packed = []
         for comp in range(3):
             ue = extrap[comp]
             flipped = [subs(ue[t], 4) for t in range(8)]
+            along_a = [None] * 8
+            for half in range(2):
+                for a, value in enumerate(slope_along([ue[2 * o + half] for o in range(4)])):
+                    along_a[2 * a + half] = value
             tiles = []
             for t in range(8):
                 a, half = t // 2, t % 2
-                along_a = combine(SLOPE[a], [ue[2 * o + half] for o in range(4)])
                 along_b = (
                     same[half][0] * ue[2 * a]
                     + cross[half][0] * flipped[2 * a]
@@ -167,41 +218,32 @@
                 )
                 along_c = spin[0] * ue[t]
                 for k in range(1, 4):
-                    moved = jnp.where(c_at + k < 4, subs(ue[t], -k), subs(ue[t], 4 - k))
-                    along_c = along_c + spin[k] * moved
-                advect = wind[0][t] * along_a + wind[1][t] * along_b + wind[2][t] * along_c
-                base = (
-                    3.0 * level(0, comp, t)
-                    - 1.5 * level(1, comp, t)
-                    + level(2, comp, t) * F32(1.0 / 3.0)
-                )
+                    along_c = along_c + spin[k] * subs(jnp.where(c_at < k, flipped[t], ue[t]), -k)
+                advect = wind[0][t] * along_a[t] + wind[1][t] * along_b + wind[2][t] * along_c
+                base = ue[t] + 1.5 * level(1, comp, t) - F32(2.0 / 3.0) * level(2, comp, t)
                 tiles.append(base + advect)
-            packed.append(swap_groups(tiles, group))
-
-        for piece in range(8):
-            flow, slot = places[piece]
-            rank = count[flow]
-
-            @pl.when(flow != me)
-            def _(flow=flow, slot=slot, rank=rank, piece=piece):
-                count[flow] = rank + 1
-                row = pl.multiple_of(flow * PEER_ROWS + rank * BLOCK_ROWS, ROWS)
-                for comp in range(3):
-                    send[pl.ds(row + comp * ROWS, ROWS), :] = packed[comp][piece]
-                mark = pl.multiple_of(flow * PEER_ROWS + CAP * BLOCK_ROWS, ROWS)
-                old = send[pl.ds(mark, ROWS), :]
-                here = (sub == 0) & (lane == CAP * me + rank)
-                send[pl.ds(mark, ROWS), :] = jnp.where(here, (slot + 1).astype(F32), old)
-
-            @pl.when(flow == me)
-            def _(slot=slot, piece=piece):
-                row = pl.multiple_of(slot * BLOCK_ROWS, ROWS)
-                for comp in range(3):
-                    keep[pl.ds(row + comp * ROWS, ROWS), :] = packed[comp][piece]
-
-        return carry
-
-    lax.fori_loop(0, columns, column, 0)
+            for (to_send, to_keep), tile in zip(places, swap_groups(tiles, group)):
+                send[pl.ds(pl.multiple_of(to_send + comp * ROWS, ROWS), ROWS), :] = tile
+                keep[pl.ds(pl.multiple_of(to_keep + comp * ROWS, ROWS), ROWS), :] = tile
+
+    @pl.loop(0, CHUNKS)
+    def _(n):
+        chunk(n).wait()
+        for k in range(columns):
+            column(n * columns + k)
+        kept(n).start()
+
+    corner = sub == 0
+    for t in range(peers):
+        marks = jnp.zeros((ROWS, 128), jnp.int32)
+        for rank in range(CAP):
+            marks = jnp.where(corner & (lane == CAP * me + rank), labels[t * CAP + rank], marks)
+        send[pl.ds(t * PEER_ROWS + CAP * BLOCK_ROWS, ROWS), :] = marks.astype(F32)
+    leaving = pltpu.make_async_copy(send, send_h, small_sem.at[0])
+    leaving.start()
+    for n in range(CHUNKS):
+        kept(n).wait()
+    leaving.wait()
 
 
 def at(a, b, c, h):
@@ -259,50 +301,45 @@
 
 
 def load_kernel(
-    len_axial, len_azim, len_radial, solid, arrived, keep, pred, part, up, down, blocks, marks, marks_s, sem, sem2
+    ids, len_axial, len_azim, len_radial, solid, arrived, keep, pred, part, up, down,
+    marks, marks_s, source, sem,
 ):
     lane, sub = iotas()
     group = lane >> 4
     peers = arrived.shape[0] // PEER_ROWS
-    fetch = pltpu.make_async_copy(keep, blocks, sem)
-    fetch.start()
     total = None
     for t in range(peers):
         tile = arrived[pl.ds(t * PEER_ROWS + CAP * BLOCK_ROWS, ROWS), :]
         total = tile if total is None else total + tile
     marks[...] = total.astype(jnp.int32)
-    scalars = pltpu.make_async_copy(marks, marks_s, sem2)
+    scalars = pltpu.make_async_copy(marks, marks_s, sem)
     scalars.start()
+    slab, sectors = lax.axis_index("stream"), lax.axis_size("azim")
+    for p in range(ids.shape[0]):
+        ident = ids[p]
+        stays = (ident >> 7) // sectors == slab
+        source[jnp.where(stays, ident & 127, 128)] = -1 - p * BLOCK_ROWS
     scalars.wait()
-    fetch.wait()
-
-    def place(n, carry):
+    for n in range(peers * CAP):
         label = marks_s[0, n]
-
-        @pl.when(label > 0)
-        def _():
-            target = pl.multiple_of((label - 1) * BLOCK_ROWS, ROWS)
-            source = pl.multiple_of((n // CAP) * PEER_ROWS + (n % CAP) * BLOCK_ROWS, ROWS)
-            for comp in range(3):
-                blocks[pl.ds(target + comp * ROWS, ROWS), :] = arrived[
-                    pl.ds(source + comp * ROWS, ROWS), :
-                ]
-
-        return carry
-
-    lax.fori_loop(0, peers * CAP, place, 0)
+        source[jnp.where(label > 0, label - 1, 128)] = (
+            (n // CAP) * PEER_ROWS + (n % CAP) * BLOCK_ROWS
+        )
 
     def unpack(j, carry):
+        places = [source[j * 8 + g] for g in range(8)]
         for comp in range(3):
-            tiles = [
-                blocks[pl.ds(pl.multiple_of((j * 8 + g) * BLOCK_ROWS, ROWS) + comp * ROWS, ROWS), :]
-                for g in range(8)
-            ]
+            tiles = []
+            for g, place in enumerate(places):
+                row = pl.multiple_of(jnp.maximum(-1 - place, 0) + comp * ROWS, ROWS)
+                kept = keep[pl.ds(row, ROWS), :]
+                row = pl.multiple_of(jnp.maximum(place, 0) + comp * ROWS, ROWS)
+                tiles.append(jnp.where(place >= 0, arrived[pl.ds(row, ROWS), :], kept))
             for t, tile in enumerate(swap_groups(tiles, group)):
                 pred[pl.ds(comp * 1024 + 8 * t * 16 + j, ROWS, stride=16), :] = tile
         return carry
 
-    lax.fori_loop(0, 16, unpack, 0)
+    lax.fori_loop(0, 16, unpack, 0, unroll=4)
 
     axial, azim, radial, _ = lengths(len_axial, len_azim, len_radial, sub)
     inverse = [
@@ -325,20 +362,20 @@
         for b in range(4):
             for c in range(4):
                 line = [scaled(0, a, b, c, h) for a in range(4)]
-                for a in range(4):
-                    part[at(a, b, c, h), :] = area[0][h] * combine(SLOPE[a], line)
+                for a, value in enumerate(slope_along(line)):
+                    part[at(a, b, c, h), :] = area[0][h] * value
         for a in range(4):
             for c in range(4):
                 line = [scaled(1, a, b, c, h) for b in range(4)]
-                for b in range(4):
-                    part[at(a, b, c, h), :] += area[1][h] * combine(SLOPE[b], line)
+                for b, value in enumerate(slope_along(line)):
+                    part[at(a, b, c, h), :] += area[1][h] * value
         for a in range(4):
             for b in range(4):
                 line = [scaled(2, a, b, c, h) for c in range(4)]
                 line = [
                     float(-WEIGHT[a] * WEIGHT[b] * WEIGHT[c])
-                    * (part[at(a, b, c, h), :] + area[2][h] * combine(SLOPE[c], line))
-                    for c in range(4)
+                    * (part[at(a, b, c, h), :] + area[2][h] * value)
+                    for c, value in enumerate(slope_along(line))
                 ]
                 for c, value in enumerate(join_radial(line, lane)):
                     part[at(a, b, c, h), :] = value
@@ -472,8 +509,8 @@
         for b in range(4):
             for c in range(4):
                 line = [field[at(a, b, c, h), :] for a in range(4)]
-                for a in range(4):
-                    value = factor[b] * combine(STIFF[a], line)
+                for a, value in enumerate(stiff_along(line)):
+                    value = factor[b] * value
                     if a == edge_a:
                         value = value + extra[b] * normals[pl.ds((b * 4 + c) * ROWS, ROWS), :]
                     image[at(a, b, c, h), :] = float(WEIGHT[b] * WEIGHT[c]) * value
@@ -483,8 +520,8 @@
             for c in range(4):
                 line = [field[at(a, b, c, h), :] for b in range(4)]
                 side = sides[pl.ds(((a * 4 + c) * 2 + h) * ROWS, ROWS), :]
-                for b in range(4):
-                    value = factor_a * combine(STIFF[b], line)
+                for b, value in enumerate(stiff_along(line)):
+                    value = factor_a * value
                     if b in (0, 3):
                         value = value + extra_a[b] * side
                     image[at(a, b, c, h), :] += float(WEIGHT[a] * WEIGHT[c]) * value
@@ -493,8 +530,8 @@
                 factor_ab = (float(WEIGHT[a] * WEIGHT[b]) * rz) * qx[h][a] * qy[b]
                 line = [field[at(a, b, c, h), :] for c in range(4)]
                 line = [
-                    image[at(a, b, c, h), :] + factor_ab * combine(STIFF[c], line)
-                    for c in range(4)
+                    image[at(a, b, c, h), :] + factor_ab * value
+                    for c, value in enumerate(stiff_along(line))
                 ]
                 for c, value in enumerate(join_radial(line, lane)):
                     image[at(a, b, c, h), :] = value
@@ -530,8 +567,8 @@
                 )
                 for axis, line in enumerate(lines):
                     dot = None
-                    for k in range(4):
-                        term = line[k] * combine(STIFF[k], line)
+                    for one, two in zip(line, stiff_along(line)):
+                        term = one * two
                         dot = term if dot is None else dot + term
                     along[axis] = along[axis] + weight * dot
         energy = (
@@ -548,7 +585,9 @@
         sums[pl.ds(k * ROWS, ROWS), :] = row
 
 
-def final_kernel(len_axial, len_azim, len_radial, sums, field, image, pred, velocity, pressure):
+def final_kernel(
+    len_axial, len_azim, len_radial, sums, field, image, pred, velocity_h, pressure_h, velocity, pressure, sems
+):
     lane, sub = iotas()
     total = sums[pl.ds(0, ROWS), :]
     for k in range(1, sums.shape[0] // ROWS):
@@ -575,46 +614,47 @@
                 for c in range(4):
                     spot = at(a, b, c, h)
                     pressure[spot, :] = of_load * field[spot, :] + of_image * image[spot, :]
-    for h in range(2):
-        scales = (2.0 / axial[h], 2.0 / azim, 2.0 / radial)
-        for m in range(4):
-            for n in range(4):
-                lines = (
-                    [(k, m, n) for k in range(4)],
-                    [(m, k, n) for k in range(4)],
-                    [(m, n, k) for k in range(4)],
-                )
-                for axis, line in enumerate(lines):
-                    values = [pressure[at(*node, h), :] for node in line]
-                    for k, (a, b, c) in enumerate(line):
+    leaving = [pltpu.make_async_copy(pressure, pressure_h, sems.at[3])]
+    leaving[0].start()
+    for axis in range(3):
+        for h in range(2):
+            scale = 2.0 / (axial[h], azim, radial)[axis]
+            for m in range(4):
+                for n in range(4):
+                    line = [(k, m, n) if axis == 0 else (m, k, n) if axis == 1 else (m, n, k) for k in range(4)]
+                    values = slope_along([pressure[at(*node, h), :] for node in line])
+                    for (a, b, c), value in zip(line, values):
                         spot = pl.ds(axis * 1024 + (a * 16 + b * 4 + c) * 16 + h * ROWS, ROWS)
-                        velocity[spot, :] = pred[spot, :] - scales[axis] * combine(
-                            SLOPE[k], values
-                        )
+                        velocity[spot, :] = pred[spot, :] - scale * value
+        span = pl.ds(axis * 1024, 1024)
+        leaving.append(pltpu.make_async_copy(velocity.at[span, :], velocity_h.at[span, :], sems.at[axis]))
+        leaving[-1].start()
+    for copy in leaving:
+        copy.wait()
 
 
 SMEM = pl.BlockSpec(memory_space=pltpu.SMEM)
 VMEM = pl.BlockSpec(memory_space=pltpu.VMEM)
-ANY = pl.BlockSpec(memory_space=pl.ANY)
+HBM = pl.BlockSpec(memory_space=pltpu.HBM)
 
 
 def array(rows, kind=F32):
     return jax.ShapeDtypeStruct((rows, 128), kind)
 
 
-def call(kernel, ins, outs, scratch, name):
+def call(kernel, ins, outs, scratch, name, place=VMEM, limit=VMEM_LIMIT):
     return pl.pallas_call(
         kernel,
         out_shape=outs,
         in_specs=ins,
-        out_specs=[VMEM] * len(outs),
+        out_specs=[place] * len(outs),
         scratch_shapes=scratch,
-        compiler_params=pltpu.CompilerParams(vmem_limit_bytes=VMEM_LIMIT),
+        compiler_params=pltpu.CompilerParams(vmem_limit_bytes=limit),
         name=name,
     )
 
 
-def around(axis, value, shift):
+def shifted(axis, value, shift):
     count = lax.axis_size(axis)
     return lax.ppermute(value, axis, [(i, (i + shift) % count) for i in range(count)])
 
@@ -624,46 +664,46 @@
     radial = len_radial.reshape(1, 128)
     geometry = (len_axial, len_azim, radial)
     geometry_specs = [SMEM, SMEM, VMEM]
-    steps = 4
     hist = history.reshape(576, history.shape[3])
-    send, keep = pl.pallas_call(
+    send, keep = call(
         pack_kernel,
-        grid=(steps,),
-        out_shape=[array(slabs * PEER_ROWS), array(128 * BLOCK_ROWS)],
-        in_specs=[
-            SMEM,
-            SMEM,
-            SMEM,
-            pl.BlockSpec((1, 128), lambda i: (0, 0)),
-            pl.BlockSpec((576, hist.shape[1] // steps), lambda i: (0, i)),
+        [HBM] * 5,
+        [array(slabs * PEER_ROWS), array(128 * BLOCK_ROWS)],
+        [
+            pltpu.VMEM(hist.shape, F32),
+            pltpu.VMEM((slabs * PEER_ROWS, 128), F32),
+            pltpu.VMEM((128 * BLOCK_ROWS, 128), F32),
+            pltpu.SMEM(block_ids.shape, jnp.int32),
+            pltpu.SMEM(len_axial.shape, F32),
+            pltpu.SMEM(len_azim.shape, F32),
+            pltpu.VMEM((1, 128), F32),
+            pltpu.SMEM((slabs,), jnp.int32),
+            pltpu.SMEM((CAP * slabs + 1,), jnp.int32),
+            pltpu.VMEM((ROWS, 128), F32),
+            pltpu.SemaphoreType.DMA((CHUNKS,)),
+            pltpu.SemaphoreType.DMA((CHUNKS,)),
+            pltpu.SemaphoreType.DMA((4,)),
         ],
-        out_specs=[
-            pl.BlockSpec((slabs * PEER_ROWS, 128), lambda i: (0, 0)),
-            pl.BlockSpec((128 * BLOCK_ROWS, 128), lambda i: (0, 0)),
-        ],
-        scratch_shapes=[pltpu.SMEM((slabs,), jnp.int32), pltpu.VMEM((ROWS, 128), F32)],
-        compiler_params=pltpu.CompilerParams(
-            vmem_limit_bytes=VMEM_LIMIT, dimension_semantics=("arbitrary",)
-        ),
-        name="pack",
-    )(block_ids, len_axial, len_azim, radial, hist)
+        "pack",
+        HBM,
+        limit=PACK_LIMIT,
+    )(block_ids, *geometry, hist)
     arrived = lax.all_to_all(
         send.reshape(slabs, PEER_ROWS, 128), "stream", split_axis=0, concat_axis=0, tiled=True
     ).reshape(slabs * PEER_ROWS, 128)
     pred, part, up, down = call(
         load_kernel,
-        geometry_specs + [VMEM, VMEM, ANY],
+        [SMEM] + geometry_specs + [VMEM] * 3,
         [array(3 * 1024), array(1024), array(128), array(128)],
         [
-            pltpu.VMEM((128 * BLOCK_ROWS, 128), F32),
             pltpu.VMEM((ROWS, 128), jnp.int32),
             pltpu.SMEM((ROWS, 128), jnp.int32),
-            pltpu.SemaphoreType.DMA(()),
+            pltpu.SMEM((129,), jnp.int32),
             pltpu.SemaphoreType.DMA(()),
         ],
         "load",
-    )(*geometry, solid.reshape(16, 128), arrived, keep)
-    below, above = around("stream", up, 1), around("stream", down, -1)
+    )(block_ids, *geometry, solid.reshape(16, 128), arrived, keep)
+    below, above = shifted("stream", up, 1), shifted("stream", down, -1)
     part, normals, up, down = call(
         axial_kernel,
         [VMEM] * 3,
@@ -671,7 +711,7 @@
         [],
         "axial_faces",
     )(part, below, above)
-    below, above = around("azim", up, 1), around("azim", down, -1)
+    below, above = shifted("azim", up, 1), shifted("azim", down, -1)
     field, image, sums = call(
         image_kernel,
         geometry_specs + [VMEM] * 4,
@@ -690,8 +730,13 @@
         final_kernel,
         geometry_specs + [VMEM] * 4,
         [array(3 * 1024), array(1024)],
-        [],
+        [
+            pltpu.VMEM((3 * 1024, 128), F32),
+            pltpu.VMEM((1024, 128), F32),
+            pltpu.SemaphoreType.DMA((4,)),
+        ],
         "velocity",
+        HBM,
     )(*geometry, sums, field, image, pred)
     return velocity.reshape(3, 4, 4, 4, 4, 4, 128), pressure.reshape(4, 4, 4, 4, 4, 128)
 

time: 79.8 us -> 70.9 us (0.89)
  local copies, waits for them, and re-layouts: 4.97 us -> 0.04 us
  Pallas kernels: 18.8 us -> 14.7 us
    unnamed x18 -> x12, local copies, waits for them, and re-layouts: 4.97 us -> 0.04 us
    pallas_call x2, Pallas kernels: 14.6 us -> 10.8 us  [the longest x1 6.48 us: body(): call(pack_kernel, [HBM] * 5, [array(slabs * PEER_ROWS), array(128 * BLOCK...]
where the time goes in v2:
time: 70.9 us; the launch traced here: 70.7 us
  blocking collectives  46.5 us (66%)
  Pallas kernels  14.7 us (21%)
  waiting for transfers between devices  5.38 us (8%)
  starting transfers between devices  3.39 us (5%)
  between operations  0.73 us (1%)
    all_to_all x1, blocking collectives, body(): lax.all_to_all(send.reshape(slabs, PEER_ROWS, 128), 'stream', split_axis=...  25.5 us
    all_to_all x1, blocking collectives, body(): lax.all_to_all(sums.reshape(slabs * sectors, 1, 128), ('stream', 'azim'),...  20.9 us
    pallas_call x1, Pallas kernels, body(): call(pack_kernel, [HBM] * 5, [array(slabs * PEER_ROWS), array(128 * BLOCK...  6.48 us
    ppermute x4, waiting for transfers between devices, shifted(): lax.ppermute(value, axis, [(i, (i + shift) % count) for i in range(count)])  5.38 us
    pallas_call x1, Pallas kernels, body(): call(load_kernel, [SMEM] + geometry_specs + [VMEM] * 3, [array(3 * 1024),...  4.31 us
    ppermute x4, starting transfers between devices, shifted(): lax.ppermute(value, axis, [(i, (i + shift) % count) for i in range(count)])  3.39 us
    pallas_call x1, Pallas kernels, body(): call(final_kernel, geometry_specs + [VMEM] * 4, [array(3 * 1024), array(1...  2.09 us
    pallas_call x1, Pallas kernels, body(): call(image_kernel, geometry_specs + [VMEM] * 4, [array(1024), array(1024)...  1.65 us
  transfers between devices with their start and end apart: 4, of which 3 were waited for; matrix products, arithmetic and copies ran while one was open for 0% of the time, Pallas kernels for 0%

profile of v2, /device:TPU:1, one launch (start us, length us, event | category | flops | bytes accessed | tf_op | source)
XLA Modules:
  0.0 70.7 jit_solution(10055651037140401001)
XLA Ops:
  0.6 6.5 %pack.1 = (f32[1792,128]{1,0:T(8,128)}, f32[3072,128]{1,0:T(8,128)}) custom-call(s32[128]{0:T(128)} %ids.1, f32[128]{0:T(128)} %len_axial.5, f32[16]{0:T(128)} %len_azim.5, f32[1,128]{1,0:T(1,128)} %bitcast.15, f32[576,2048]{1,0:T(8,128)} %bitcast.19), custom_call_target="tpu_custom_call" | custom-call | tf_op jit(solution)/shard_map/pack/pallas_call | solution.py:668
  7.1 0.0 copy-start
  7.1 0.0 copy-start.1
  7.1 0.0 copy-start.2
  7.2 0.0 copy-start.3
  7.2 0.0 copy-start.4
  7.2 0.0 copy-start.5
  7.2 25.5 %all_to_all.10 = f32[32,56,128]{2,1,0:T(8,128)S(1)} all-to-all(f32[32,56,128]{2,1,0:T(8,128)} %bitcast.20), channel_id=1, replica_groups=mesh['stream'=32,'azim'=4] {'stream'}, dimensions={0} | all-to-all | bytes 1835008 | tf_op jit(solution)/shard_map/all_to_all | solution.py:691
  32.7 0.0 copy-done
  32.7 0.0 copy-done.1
  32.7 0.0 copy-done.2
  32.7 0.0 copy-done.3
  32.7 0.0 copy-done.4
  32.7 0.0 copy-done.5
  32.7 4.3 %load.1 = (f32[3072,128]{1,0:T(8,128)S(1)}, f32[1024,128]{1,0:T(8,128)S(1)}, f32[128,128]{1,0:T(8,128)S(1)}, f32[128,128]{1,0:T(8,128)S(1)}) custom-call(s32[128]{0:T(128)S(1)} %copy-done.5, f32[128]{0:T(128)S(1)} %copy-done.2, f32[16]{0:T(128)S(1)} %copy-done.3, f32[1,128]{1,0:T(1,128)S(1)} %bitcast.16, s32[16,128]{1,0:T(8,128)S(1)} %bitcast.14, ...), custom_call_target="tpu_custom_call" | custom-call | tf_op jit(solution)/shard_map/load/pallas_call | solution.py:694
  37.0 0.6 collective-permute-start
  37.7 0.0 collective-permute-start.1
  37.7 1.3 %collective-permute-done.below = f32[128,128]{1,0:T(8,128)S(1)} collective-permute-done((f32[128,128]{1,0:T(8,128)S(1)}, f32[128,128]{1,0:T(8,128)S(1)}, u32[]{:S(2)}, u32[]{:S(2)}) %collective-permute-start) | collective-permute-done | bytes 65568 | tf_op jit(solution)/shard_map/ppermute | solution.py:659
  39.0 2.4 %collective-permute-done.1.above = f32[128,128]{1,0:T(8,128)S(1)} collective-permute-done((f32[128,128]{1,0:T(8,128)S(1)}, f32[128,128]{1,0:T(8,128)S(1)}, u32[]{:S(2)}, u32[]{:S(2)}) %collective-permute-start.1) | collective-permute-done | bytes 65568 | tf_op jit(solution)/shard_map/ppermute | solution.py:659
  41.4 0.1 axial_faces.1
  41.5 1.3 %collective-permute-start.2 = (f32[136,128]{1,0:T(8,128)S(1)}, f32[136,128]{1,0:T(8,128)S(1)}, u32[]{:S(2)}, u32[]{:S(2)}) collective-permute-start(f32[136,128]{1,0:T(8,128)S(1)} %get-tuple-element.24), channel_id=1, source_target_pairs={{0,1},{1,2},{2,3},{3,0},{4,5},{5,6},{6,7},{7,4},{8,9},{9,10},{10,1... | collective-permute-start | bytes 208904 | tf_op jit(solution)/shard_map/ppermute | solution.py:659
  42.8 1.5 %collective-permute-start.3 = (f32[136,128]{1,0:T(8,128)S(1)}, f32[136,128]{1,0:T(8,128)S(1)}, u32[]{:S(2)}, u32[]{:S(2)}) collective-permute-start(f32[136,128]{1,0:T(8,128)S(1)} %get-tuple-element.25), channel_id=1, source_target_pairs={{0,3},{1,0},{2,1},{3,2},{4,7},{5,4},{6,5},{7,6},{8,11},{9,8},{10,9... | collective-permute-start | bytes 208904 | tf_op jit(solution)/shard_map/ppermute | solution.py:659
  44.3 1.7 %collective-permute-done.2.below = f32[136,128]{1,0:T(8,128)S(1)} collective-permute-done((f32[136,128]{1,0:T(8,128)S(1)}, f32[136,128]{1,0:T(8,128)S(1)}, u32[]{:S(2)}, u32[]{:S(2)}) %collective-permute-start.2) | collective-permute-done | bytes 69664 | tf_op jit(solution)/shard_map/ppermute | solution.py:659
  46.0 0.0 collective-permute-done.3.above
  46.0 1.7 %image.1 = (f32[1024,128]{1,0:T(8,128)S(1)}, f32[1024,128]{1,0:T(8,128)S(1)}, f32[128,128]{1,0:T(8,128)S(1)}) custom-call(f32[128]{0:T(128)S(1)} %copy-done.2, f32[16]{0:T(128)S(1)} %copy-done.3, f32[1,128]{1,0:T(1,128)S(1)} %bitcast.17, f32[1024,128]{1,0:T(8,128)S(1)} %get-tuple-element.22.part, f32[128,128]{1,0:T(8,128)S(1)} %get-tuple-element.23.normals_in, ...), custom_call_target="tpu_custom_call" | custom-call | tf_op jit(solution)/shard_map/image/pallas_call | solution.py:715
  47.6 20.9 %all_to_all.11 = f32[128,1,128]{2,1,0:T(1,128)S(1)} all-to-all(f32[128,1,128]{2,1,0:T(1,128)S(1)} %bitcast.13), channel_id=1, replica_groups=mesh['stream'=32,'azim'=4] {'stream','azim'}, dimensions={0} | all-to-all | bytes 131072 | tf_op jit(solution)/shard_map/all_to_all | solution.py:722
  68.6 2.1 %velocity.1 = (f32[3072,128]{1,0:T(8,128)}, f32[1024,128]{1,0:T(8,128)}) custom-call(f32[128]{0:T(128)S(1)} %copy-done.2, f32[16]{0:T(128)S(1)} %copy-done.3, f32[1,128]{1,0:T(1,128)S(1)} %bitcast.18, f32[128,128]{1,0:T(8,128)S(1)} %bitcast.12, f32[1024,128]{1,0:T(8,128)S(1)} %get-tuple-element.27.field, f32[1024,128]{1,0:T(8,128)S(1)} %get-tuple-element.28.image, ...), custom_call_target="tpu_custom_call" | custom-call | tf_op jit(solution)/shard_map/velocity/pallas_call | solution.py:729
Async XLA Ops:
  7.1 25.6 %copy-start = (f32[3072,128]{1,0:T(8,128)S(1)}, f32[3072,128]{1,0:T(8,128)}, u32[]{:S(2)}) copy-start(f32[3072,128]{1,0:T(8,128)} %get-tuple-element.18.keep) | copy-start | bytes 4718596
  7.1 25.6 %copy-start.1 = (s32[4,4,128]{2,1,0:T(4,128)S(1)}, s32[4,4,128]{2,1,0:T(4,128)}, u32[]{:S(2)}) copy-start(s32[4,4,128]{2,1,0:T(4,128)} %param.11) | copy-start | bytes 24580
  7.1 25.6 %copy-start.2 = (f32[128]{0:T(128)S(1)}, f32[128]{0:T(128)}, u32[]{:S(2)}) copy-start(f32[128]{0:T(128)} %len_axial.5) | copy-start | bytes 1540
  7.2 25.6 %copy-start.3 = (f32[16]{0:T(128)S(1)}, f32[16]{0:T(128)}, u32[]{:S(2)}) copy-start(f32[16]{0:T(128)} %len_azim.5) | copy-start | bytes 196
  7.2 25.6 %copy-start.4 = (f32[128]{0:T(128)S(1)}, f32[128]{0:T(128)}, u32[]{:S(2)}) copy-start(f32[128]{0:T(128)} %param.10) | copy-start | bytes 1540
  7.2 25.6 %copy-start.5 = (s32[128]{0:T(128)S(1)}, s32[128]{0:T(128)}, u32[]{:S(2)}) copy-start(s32[128]{0:T(128)} %ids.1) | copy-start | bytes 1540
  37.0 2.0 %collective-permute-start = (f32[128,128]{1,0:T(8,128)S(1)}, f32[128,128]{1,0:T(8,128)S(1)}, u32[]{:S(2)}, u32[]{:S(2)}) collective-permute-start(f32[128,128]{1,0:T(8,128)S(1)} %get-tuple-element.20), channel_id=1, source_target_pairs={{0,4},{4,8},{8,12},{12,16},{16,20},{20,24},{24,28},{28,32},{32,36}... | collective-permute-start | bytes 196616 | tf_op jit(solution)/shard_map/ppermute | solution.py:659
  37.7 3.7 %collective-permute-start.1 = (f32[128,128]{1,0:T(8,128)S(1)}, f32[128,128]{1,0:T(8,128)S(1)}, u32[]{:S(2)}, u32[]{:S(2)}) collective-permute-start(f32[128,128]{1,0:T(8,128)S(1)} %get-tuple-element.21), channel_id=1, source_target_pairs={{0,124},{4,0},{8,4},{12,8},{16,12},{20,16},{24,20},{28,24},{32,28}... | collective-permute-start | bytes 196616 | tf_op jit(solution)/shard_map/ppermute | solution.py:659
  41.5 4.4 %collective-permute-start.2 = (f32[136,128]{1,0:T(8,128)S(1)}, f32[136,128]{1,0:T(8,128)S(1)}, u32[]{:S(2)}, u32[]{:S(2)}) collective-permute-start(f32[136,128]{1,0:T(8,128)S(1)} %get-tuple-element.24), channel_id=1, source_target_pairs={{0,1},{1,2},{2,3},{3,0},{4,5},{5,6},{6,7},{7,4},{8,9},{9,10},{10,1... | collective-permute-start | bytes 208904 | tf_op jit(solution)/shard_map/ppermute | solution.py:659
  42.8 3.2 %collective-permute-start.3 = (f32[136,128]{1,0:T(8,128)S(1)}, f32[136,128]{1,0:T(8,128)S(1)}, u32[]{:S(2)}, u32[]{:S(2)}) collective-permute-start(f32[136,128]{1,0:T(8,128)S(1)} %get-tuple-element.25), channel_id=1, source_target_pairs={{0,3},{1,0},{2,1},{3,2},{4,7},{5,4},{6,5},{7,6},{8,11},{9,8},{10,9... | collective-permute-start | bytes 208904 | tf_op jit(solution)/shard_map/ppermute | solution.py:659

commit v3 on v2

--- a/solution.py
+++ b/solution.py
@@ -300,8 +300,18 @@
     return axial, azim, radial, (before, after, below, above)
 
 
+def give(near, far, row, even, up, down):
+    near[pl.ds(row, ROWS), :] = jnp.where(even, up, down)
+    far[pl.ds(row, ROWS), :] = jnp.where(even, down, up)
+
+
+def take(near, far, row, even):
+    one, two = near[pl.ds(row, ROWS), :], far[pl.ds(row, ROWS), :]
+    return jnp.where(even, two, one), jnp.where(even, one, two)
+
+
 def load_kernel(
-    ids, len_axial, len_azim, len_radial, solid, arrived, keep, pred, part, up, down,
+    ids, len_axial, len_azim, len_radial, solid, arrived, keep, pred, part, near, far,
     marks, marks_s, source, sem,
 ):
     lane, sub = iotas()
@@ -381,6 +391,7 @@
                     part[at(a, b, c, h), :] = value
     join_azim(part, sub)
     top = sub < 4
+    even = lax.rem(slab, 2) == 0
     for b in range(4):
         for c in range(4):
             low, high = join_axial(part, b, c, sub)
@@ -388,25 +399,26 @@
                 part[at(0, b, c, h), :] = low[h]
                 part[at(3, b, c, h), :] = high[h]
             inner = [[part[at(a, b, c, h), :] for a in (1, 2)] for h in range(2)]
-            spot = pl.ds((b * 4 + c) * ROWS, ROWS)
             normal = combine(STIFF[3], [low[1], *inner[1], high[1]])
-            up[spot, :] = jnp.where(top, subs(high[1], 4), normal)
+            up = jnp.where(top, subs(high[1], 4), normal)
             normal = combine(STIFF[0], [low[0], *inner[0], high[0]])
-            down[spot, :] = jnp.where(top, low[0], subs(normal, 4))
-
-
-def axial_kernel(part, below, above, field, normals, up, down):
+            down = jnp.where(top, low[0], subs(normal, 4))
+            give(near, far, (b * 4 + c) * ROWS, even, up, down)
+
+
+def axial_kernel(part, near_in, far_in, field, normals, near, far):
     lane, sub = iotas()
     top = sub < 4
     slab = lax.axis_index("stream")
     first = jnp.where(slab == 0, F32(0.0), F32(1.0))
     last = jnp.where(slab == lax.axis_size("stream") - 1, F32(0.0), F32(1.0))
+    even = lax.rem(slab, 2) == 0
     for b in range(4):
         for c in range(4):
             spot = pl.ds((b * 4 + c) * ROWS, ROWS)
             low = part[at(0, b, c, 0), :]
             high = part[at(3, b, c, 1), :]
-            under, over = below[spot, :], above[spot, :]
+            under, over = take(near_in, far_in, (b * 4 + c) * ROWS, even)
             normals[spot, :] = jnp.where(
                 top,
                 subs(under, 4) + float(STIFF[3, 3]) * low,
@@ -420,27 +432,28 @@
                 for h in range(2):
                     field[at(a, b, c, h), :] = part[at(a, b, c, h), :]
     ey = sub & 3
+    even = lax.rem(lax.axis_index("azim"), 2) == 0
     for a in range(4):
         for c in range(4):
-            spot = pl.ds((a * 4 + c) * ROWS, ROWS)
             line = [[field[at(a, b, c, h), :] for b in range(4)] for h in range(2)]
             normal = [combine(STIFF[3], line[h]) for h in range(2)]
-            up[spot, :] = choose(
+            up = choose(
                 ey, [subs(normal[1], -3), subs(normal[0], -2), subs(line[1][3], -1), line[0][3]]
             )
             normal = [combine(STIFF[0], line[h]) for h in range(2)]
-            down[spot, :] = choose(
+            down = choose(
                 ey, [line[0][0], subs(line[1][0], 1), subs(normal[0], 2), subs(normal[1], 3)]
             )
-    spot = pl.ds(16 * ROWS, ROWS)
+            give(near, far, (a * 4 + c) * ROWS, even, up, down)
     edge = [normals[pl.ds((12 + c) * ROWS, ROWS), :] for c in range(4)]
-    up[spot, :] = choose(ey, [subs(edge[3], -3), subs(edge[2], -2), subs(edge[1], -1), edge[0]])
+    up = choose(ey, [subs(edge[3], -3), subs(edge[2], -2), subs(edge[1], -1), edge[0]])
     edge = [normals[pl.ds(c * ROWS, ROWS), :] for c in range(4)]
-    down[spot, :] = choose(ey, [edge[0], subs(edge[1], 1), subs(edge[2], 2), subs(edge[3], 3)])
+    down = choose(ey, [edge[0], subs(edge[1], 1), subs(edge[2], 2), subs(edge[3], 3)])
+    give(near, far, 16 * ROWS, even, up, down)
 
 
 def image_kernel(
-    len_axial, len_azim, len_radial, part, normals_in, below, above, field, image, sums, normals, sides
+    len_axial, len_azim, len_radial, part, normals_in, near, far, field, image, sums, normals, sides
 ):
     lane, sub = iotas()
     top = sub < 4
@@ -448,10 +461,10 @@
     slab = lax.axis_index("stream")
     first = jnp.where(slab == 0, F32(0.0), F32(1.0))
     last = jnp.where(slab == lax.axis_size("stream") - 1, F32(0.0), F32(1.0))
+    even = lax.rem(lax.axis_index("azim"), 2) == 0
     for a in range(4):
         for c in range(4):
-            spot = pl.ds((a * 4 + c) * ROWS, ROWS)
-            under, over = below[spot, :], above[spot, :]
+            under, over = take(near, far, (a * 4 + c) * ROWS, even)
             under_face = [subs(under, -3), subs(under, -2)]
             under_normal = [subs(under, -1), under]
             over_face = [subs(over, 3), subs(over, 2)]
@@ -468,7 +481,7 @@
                 field[at(a, 3, c, h), :] = high + jnp.where(ey == 3, over_face[h], 0.0)
                 for b in (1, 2):
                     field[at(a, b, c, h), :] = part[at(a, b, c, h), :]
-    under, over = below[pl.ds(16 * ROWS, ROWS), :], above[pl.ds(16 * ROWS, ROWS), :]
+    under, over = take(near, far, 16 * ROWS, even)
     for c in range(4):
         spot = pl.ds(c * ROWS, ROWS)
         normals[spot, :] = normals_in[spot, :] + jnp.where(ey == 0, subs(under, c - 3), 0.0)
@@ -654,9 +667,13 @@
     )
 
 
-def shifted(axis, value, shift):
+def swapped(axis, near, far, closed):
     count = lax.axis_size(axis)
-    return lax.ppermute(value, axis, [(i, (i + shift) % count) for i in range(count)])
+    apart = [(i + 1) % count if i % 2 else (i - 1) % count for i in range(count)]
+    if not closed:
+        apart[0], apart[-1] = 0, count - 1
+    far = lax.ppermute(far, axis, list(enumerate(apart)))
+    return lax.ppermute(near, axis, [(i, i ^ 1) for i in range(count)]), far
 
 
 def body(history, block_ids, len_axial, len_azim, len_radial, solid):
@@ -691,7 +708,7 @@
     arrived = lax.all_to_all(
         send.reshape(slabs, PEER_ROWS, 128), "stream", split_axis=0, concat_axis=0, tiled=True
     ).reshape(slabs * PEER_ROWS, 128)
-    pred, part, up, down = call(
+    pred, part, near, far = call(
         load_kernel,
         [SMEM] + geometry_specs + [VMEM] * 3,
         [array(3 * 1024), array(1024), array(128), array(128)],
@@ -703,22 +720,22 @@
         ],
         "load",
     )(block_ids, *geometry, solid.reshape(16, 128), arrived, keep)
-    below, above = shifted("stream", up, 1), shifted("stream", down, -1)
-    part, normals, up, down = call(
+    near, far = swapped("stream", near, far, False)
+    part, normals, near, far = call(
         axial_kernel,
         [VMEM] * 3,
         [array(1024), array(128), array(136), array(136)],
         [],
         "axial_faces",
-    )(part, below, above)
-    below, above = shifted("azim", up, 1), shifted("azim", down, -1)
+    )(part, near, far)
+    near, far = swapped("azim", near, far, True)
     field, image, sums = call(
         image_kernel,
         geometry_specs + [VMEM] * 4,
         [array(1024), array(1024), array(slabs * sectors)],
         [pltpu.VMEM((128, 128), F32), pltpu.VMEM((256, 128), F32)],
         "image",
-    )(*geometry, part, normals, below, above)
+    )(*geometry, part, normals, near, far)
     sums = lax.all_to_all(
         sums.reshape(slabs * sectors, 1, 128),
         ("stream", "azim"),

time: 70.9 us -> 69.8 us (0.984)
  blocking collectives: 46.5 us -> 42.1 us
  starting transfers between devices: 3.39 us -> 6.18 us
    all_to_all x1, blocking collectives: 20.9 us -> 16.6 us  [body(): lax.all_to_all(sums.reshape(slabs * sectors, 1, 128), ('stream', 'azim'),...]
    ppermute x4, starting transfers between devices: 3.39 us -> 6.18 us  [the longest x2 4.12 us: swapped(): far = lax.ppermute(far, axis, list(enumerate(apart)))]
  transfers between devices with their start and end apart: 4 -> 4, of which waited for: 3 -> 2; matrix products, arithmetic and copies ran while one was open for 0% -> 0% of each run, Pallas kernels for 0% -> 0%
where the time goes in v3:
time: 69.8 us; the launch traced here: 69.6 us
  blocking collectives  42.1 us (60%)
  Pallas kernels  14.7 us (21%)
  starting transfers between devices  6.18 us (9%)
  waiting for transfers between devices  5.8 us (8%)
  between operations  0.74 us (1%)
    all_to_all x1, blocking collectives, body(): lax.all_to_all(send.reshape(slabs, PEER_ROWS, 128), 'stream', split_axis=...  25.5 us
    all_to_all x1, blocking collectives, body(): lax.all_to_all(sums.reshape(slabs * sectors, 1, 128), ('stream', 'azim'),...  16.6 us
    pallas_call x1, Pallas kernels, body(): call(pack_kernel, [HBM] * 5, [array(slabs * PEER_ROWS), array(128 * BLOCK...  6.48 us
    ppermute x2, waiting for transfers between devices, swapped(): far = lax.ppermute(far, axis, list(enumerate(apart)))  5.8 us
    pallas_call x1, Pallas kernels, body(): call(load_kernel, [SMEM] + geometry_specs + [VMEM] * 3, [array(3 * 1024),...  4.31 us
    ppermute x2, starting transfers between devices, swapped(): far = lax.ppermute(far, axis, list(enumerate(apart)))  4.12 us
    pallas_call x1, Pallas kernels, body(): call(final_kernel, geometry_specs + [VMEM] * 4, [array(3 * 1024), array(1...  2.09 us
    ppermute x2, starting transfers between devices, swapped(): return (lax.ppermute(near, axis, [(i, i ^ 1) for i in range(count)]), far)  2.06 us
  transfers between devices with their start and end apart: 4, of which 2 were waited for; matrix products, arithmetic and copies ran while one was open for 0% of the time, Pallas kernels for 0%

profile of v3, /device:TPU:1, one launch (start us, length us, event | category | flops | bytes accessed | tf_op | source)
XLA Modules:
  0.0 69.6 jit_solution(11367339427603824608)
XLA Ops:
  0.6 6.5 %pack.1 = (f32[1792,128]{1,0:T(8,128)}, f32[3072,128]{1,0:T(8,128)}) custom-call(s32[128]{0:T(128)} %ids.1, f32[128]{0:T(128)} %len_axial.5, f32[16]{0:T(128)} %len_azim.5, f32[1,128]{1,0:T(1,128)} %bitcast.15, f32[576,2048]{1,0:T(8,128)} %bitcast.19), custom_call_target="tpu_custom_call" | custom-call | tf_op jit(solution)/shard_map/pack/pallas_call | solution.py:685
  7.1 0.0 copy-start
  7.1 0.0 copy-start.1
  7.1 0.0 copy-start.2
  7.2 0.0 copy-start.3
  7.2 0.0 copy-start.4
  7.2 0.0 copy-start.5
  7.2 25.5 %all_to_all.10 = f32[32,56,128]{2,1,0:T(8,128)S(1)} all-to-all(f32[32,56,128]{2,1,0:T(8,128)} %bitcast.20), channel_id=1, replica_groups=mesh['stream'=32,'azim'=4] {'stream'}, dimensions={0} | all-to-all | bytes 1835008 | tf_op jit(solution)/shard_map/all_to_all | solution.py:708
  32.7 0.0 copy-done
  32.7 0.0 copy-done.1
  32.7 0.0 copy-done.2
  32.7 0.0 copy-done.3
  32.7 0.0 copy-done.4
  32.7 0.0 copy-done.5
  32.7 4.3 %load.1 = (f32[3072,128]{1,0:T(8,128)S(1)}, f32[1024,128]{1,0:T(8,128)S(1)}, f32[128,128]{1,0:T(8,128)S(1)}, f32[128,128]{1,0:T(8,128)S(1)}) custom-call(s32[128]{0:T(128)S(1)} %copy-done.5, f32[128]{0:T(128)S(1)} %copy-done.2, f32[16]{0:T(128)S(1)} %copy-done.3, f32[1,128]{1,0:T(1,128)S(1)} %bitcast.16, s32[16,128]{1,0:T(8,128)S(1)} %bitcast.14, ...), custom_call_target="tpu_custom_call" | custom-call | tf_op jit(solution)/shard_map/load/pallas_call | solution.py:711
  37.1 0.5 collective-permute-start
  37.5 2.3 %collective-permute-start.1 = (f32[128,128]{1,0:T(8,128)S(1)}, f32[128,128]{1,0:T(8,128)S(1)}, u32[]{:S(2)}, u32[]{:S(2)}) collective-permute-start(f32[128,128]{1,0:T(8,128)S(1)} %get-tuple-element.21), channel_id=1, source_target_pairs={{0,0},{4,8},{8,4},{12,16},{16,12},{20,24},{24,20},{28,32},{32,28},... | collective-permute-start | bytes 196616 | tf_op jit(solution)/shard_map/ppermute | solution.py:675
  39.8 0.0 collective-permute-done.near_in
  39.9 3.2 %collective-permute-done.1.far_in = f32[128,128]{1,0:T(8,128)S(1)} collective-permute-done((f32[128,128]{1,0:T(8,128)S(1)}, f32[128,128]{1,0:T(8,128)S(1)}, u32[]{:S(2)}, u32[]{:S(2)}) %collective-permute-start.1) | collective-permute-done | bytes 65568 | tf_op jit(solution)/shard_map/ppermute | solution.py:675
  43.1 0.1 axial_faces.1
  43.3 1.6 %collective-permute-start.2 = (f32[136,128]{1,0:T(8,128)S(1)}, f32[136,128]{1,0:T(8,128)S(1)}, u32[]{:S(2)}, u32[]{:S(2)}) collective-permute-start(f32[136,128]{1,0:T(8,128)S(1)} %get-tuple-element.24), channel_id=1, source_target_pairs={{0,1},{1,0},{2,3},{3,2},{4,5},{5,4},{6,7},{7,6},{8,9},{9,8},{10,11... | collective-permute-start | bytes 208904 | tf_op jit(solution)/shard_map/ppermute | solution.py:676
  44.8 1.8 %collective-permute-start.3 = (f32[136,128]{1,0:T(8,128)S(1)}, f32[136,128]{1,0:T(8,128)S(1)}, u32[]{:S(2)}, u32[]{:S(2)}) collective-permute-start(f32[136,128]{1,0:T(8,128)S(1)} %get-tuple-element.25), channel_id=1, source_target_pairs={{0,3},{1,2},{2,1},{3,0},{4,7},{5,6},{6,5},{7,4},{8,11},{9,10},{10,... | collective-permute-start | bytes 208904 | tf_op jit(solution)/shard_map/ppermute | solution.py:675
  46.7 0.0 collective-permute-done.2.near
  46.7 2.5 %collective-permute-done.3.far = f32[136,128]{1,0:T(8,128)S(1)} collective-permute-done((f32[136,128]{1,0:T(8,128)S(1)}, f32[136,128]{1,0:T(8,128)S(1)}, u32[]{:S(2)}, u32[]{:S(2)}) %collective-permute-start.3) | collective-permute-done | bytes 69664 | tf_op jit(solution)/shard_map/ppermute | solution.py:675
  49.2 1.7 %image.1 = (f32[1024,128]{1,0:T(8,128)S(1)}, f32[1024,128]{1,0:T(8,128)S(1)}, f32[128,128]{1,0:T(8,128)S(1)}) custom-call(f32[128]{0:T(128)S(1)} %copy-done.2, f32[16]{0:T(128)S(1)} %copy-done.3, f32[1,128]{1,0:T(1,128)S(1)} %bitcast.17, f32[1024,128]{1,0:T(8,128)S(1)} %get-tuple-element.22.part, f32[128,128]{1,0:T(8,128)S(1)} %get-tuple-element.23.normals_in, ...), custom_call_target="tpu_custom_call" | custom-call | tf_op jit(solution)/shard_map/image/pallas_call | solution.py:732
  50.9 16.6 %all_to_all.11 = f32[128,1,128]{2,1,0:T(1,128)S(1)} all-to-all(f32[128,1,128]{2,1,0:T(1,128)S(1)} %bitcast.13), channel_id=1, replica_groups=mesh['stream'=32,'azim'=4] {'stream','azim'}, dimensions={0} | all-to-all | bytes 131072 | tf_op jit(solution)/shard_map/all_to_all | solution.py:739
  67.5 2.1 %velocity.1 = (f32[3072,128]{1,0:T(8,128)}, f32[1024,128]{1,0:T(8,128)}) custom-call(f32[128]{0:T(128)S(1)} %copy-done.2, f32[16]{0:T(128)S(1)} %copy-done.3, f32[1,128]{1,0:T(1,128)S(1)} %bitcast.18, f32[128,128]{1,0:T(8,128)S(1)} %bitcast.12, f32[1024,128]{1,0:T(8,128)S(1)} %get-tuple-element.27.field, f32[1024,128]{1,0:T(8,128)S(1)} %get-tuple-element.28.image, ...), custom_call_target="tpu_custom_call" | custom-call | tf_op jit(solution)/shard_map/velocity/pallas_call | solution.py:746
Async XLA Ops:
  7.1 25.6 %copy-start = (f32[3072,128]{1,0:T(8,128)S(1)}, f32[3072,128]{1,0:T(8,128)}, u32[]{:S(2)}) copy-start(f32[3072,128]{1,0:T(8,128)} %get-tuple-element.18.keep) | copy-start | bytes 4718596
  7.1 25.6 %copy-start.1 = (s32[4,4,128]{2,1,0:T(4,128)S(1)}, s32[4,4,128]{2,1,0:T(4,128)}, u32[]{:S(2)}) copy-start(s32[4,4,128]{2,1,0:T(4,128)} %param.11) | copy-start | bytes 24580
  7.1 25.6 %copy-start.2 = (f32[128]{0:T(128)S(1)}, f32[128]{0:T(128)}, u32[]{:S(2)}) copy-start(f32[128]{0:T(128)} %len_axial.5) | copy-start | bytes 1540
  7.2 25.6 %copy-start.3 = (f32[16]{0:T(128)S(1)}, f32[16]{0:T(128)}, u32[]{:S(2)}) copy-start(f32[16]{0:T(128)} %len_azim.5) | copy-start | bytes 196
  7.2 25.6 %copy-start.4 = (f32[128]{0:T(128)S(1)}, f32[128]{0:T(128)}, u32[]{:S(2)}) copy-start(f32[128]{0:T(128)} %param.10) | copy-start | bytes 1540
  7.2 25.6 %copy-start.5 = (s32[128]{0:T(128)S(1)}, s32[128]{0:T(128)}, u32[]{:S(2)}) copy-start(s32[128]{0:T(128)} %ids.1) | copy-start | bytes 1540
  37.1 2.8 %collective-permute-start = (f32[128,128]{1,0:T(8,128)S(1)}, f32[128,128]{1,0:T(8,128)S(1)}, u32[]{:S(2)}, u32[]{:S(2)}) collective-permute-start(f32[128,128]{1,0:T(8,128)S(1)} %get-tuple-element.20), channel_id=1, source_target_pairs={{0,4},{4,0},{8,12},{12,8},{16,20},{20,16},{24,28},{28,24},{32,36},... | collective-permute-start | bytes 196616 | tf_op jit(solution)/shard_map/ppermute | solution.py:676
  37.5 5.6 %collective-permute-start.1 = (f32[128,128]{1,0:T(8,128)S(1)}, f32[128,128]{1,0:T(8,128)S(1)}, u32[]{:S(2)}, u32[]{:S(2)}) collective-permute-start(f32[128,128]{1,0:T(8,128)S(1)} %get-tuple-element.21), channel_id=1, source_target_pairs={{0,0},{4,8},{8,4},{12,16},{16,12},{20,24},{24,20},{28,32},{32,28},... | collective-permute-start | bytes 196616 | tf_op jit(solution)/shard_map/ppermute | solution.py:675
  43.3 3.4 %collective-permute-start.2 = (f32[136,128]{1,0:T(8,128)S(1)}, f32[136,128]{1,0:T(8,128)S(1)}, u32[]{:S(2)}, u32[]{:S(2)}) collective-permute-start(f32[136,128]{1,0:T(8,128)S(1)} %get-tuple-element.24), channel_id=1, source_target_pairs={{0,1},{1,0},{2,3},{3,2},{4,5},{5,4},{6,7},{7,6},{8,9},{9,8},{10,11... | collective-permute-start | bytes 208904 | tf_op jit(solution)/shard_map/ppermute | solution.py:676
  44.8 4.4 %collective-permute-start.3 = (f32[136,128]{1,0:T(8,128)S(1)}, f32[136,128]{1,0:T(8,128)S(1)}, u32[]{:S(2)}, u32[]{:S(2)}) collective-permute-start(f32[136,128]{1,0:T(8,128)S(1)} %get-tuple-element.25), channel_id=1, source_target_pairs={{0,3},{1,2},{2,1},{3,0},{4,7},{5,6},{6,5},{7,4},{8,11},{9,10},{10,... | collective-permute-start | bytes 208904 | tf_op jit(solution)/shard_map/ppermute | solution.py:675

commit v4 on v3

--- a/solution.py
+++ b/solution.py
@@ -349,7 +349,7 @@
                 pred[pl.ds(comp * 1024 + 8 * t * 16 + j, ROWS, stride=16), :] = tile
         return carry
 
-    lax.fori_loop(0, 16, unpack, 0, unroll=4)
+    lax.fori_loop(0, 16, unpack, 0, unroll=8)
 
     axial, azim, radial, _ = lengths(len_axial, len_azim, len_radial, sub)
     inverse = [
@@ -627,21 +627,34 @@
                 for c in range(4):
                     spot = at(a, b, c, h)
                     pressure[spot, :] = of_load * field[spot, :] + of_image * image[spot, :]
-    leaving = [pltpu.make_async_copy(pressure, pressure_h, sems.at[3])]
+    leaving = [pltpu.make_async_copy(pressure, pressure_h, sems.at[9])]
     leaving[0].start()
-    for axis in range(3):
-        for h in range(2):
-            scale = 2.0 / (axial[h], azim, radial)[axis]
-            for m in range(4):
-                for n in range(4):
-                    line = [(k, m, n) if axis == 0 else (m, k, n) if axis == 1 else (m, n, k) for k in range(4)]
-                    values = slope_along([pressure[at(*node, h), :] for node in line])
-                    for (a, b, c), value in zip(line, values):
-                        spot = pl.ds(axis * 1024 + (a * 16 + b * 4 + c) * 16 + h * ROWS, ROWS)
-                        velocity[spot, :] = pred[spot, :] - scale * value
-        span = pl.ds(axis * 1024, 1024)
-        leaving.append(pltpu.make_async_copy(velocity.at[span, :], velocity_h.at[span, :], sems.at[axis]))
+    scales = [[2.0 / (axial[h], azim, radial)[axis] for h in range(2)] for axis in range(3)]
+
+    def write(axis, line, h):
+        values = slope_along([pressure[at(*node, h), :] for node in line])
+        for (a, b, c), value in zip(line, values):
+            spot = pl.ds(axis * 1024 + (a * 16 + b * 4 + c) * 16 + h * ROWS, ROWS)
+            velocity[spot, :] = pred[spot, :] - scales[axis][h] * value
+
+    def leave(first, rows):
+        span = pl.ds(first, rows)
+        leaving.append(
+            pltpu.make_async_copy(velocity.at[span, :], velocity_h.at[span, :], sems.at[len(leaving) - 1])
+        )
         leaving[-1].start()
+
+    for m in range(4):
+        for n in range(4):
+            for h in range(2):
+                write(0, [(k, m, n) for k in range(4)], h)
+    leave(0, 1024)
+    for axis in (1, 2):
+        for a in range(4):
+            for n in range(4):
+                for h in range(2):
+                    write(axis, [(a, k, n) if axis == 1 else (a, n, k) for k in range(4)], h)
+            leave(axis * 1024 + a * 256, 256)
     for copy in leaving:
         copy.wait()
 
@@ -750,7 +763,7 @@
         [
             pltpu.VMEM((3 * 1024, 128), F32),
             pltpu.VMEM((1024, 128), F32),
-            pltpu.SemaphoreType.DMA((4,)),
+            pltpu.SemaphoreType.DMA((10,)),
         ],
         "velocity",
         HBM,

time: 69.8 us -> 70.9 us (1.016)
  Pallas kernels: 14.7 us -> 15.8 us
    pallas_call x1, Pallas kernels: 4.31 us -> 5.31 us  [body(): call(load_kernel, [SMEM] + geometry_specs + [VMEM] * 3, [array(3 * 1024),...]
where the time goes in v4:
time: 70.9 us; the launch traced here: 70.6 us
  blocking collectives  42.1 us (59%)
  Pallas kernels  15.8 us (22%)
  starting transfers between devices  6.18 us (9%)
  waiting for transfers between devices  5.8 us (8%)
  between operations  0.74 us (1%)
    all_to_all x1, blocking collectives, body(): lax.all_to_all(send.reshape(slabs, PEER_ROWS, 128), 'stream', split_axis=...  25.5 us
    all_to_all x1, blocking collectives, body(): lax.all_to_all(sums.reshape(slabs * sectors, 1, 128), ('stream', 'azim'),...  16.6 us
    pallas_call x1, Pallas kernels, body(): call(pack_kernel, [HBM] * 5, [array(slabs * PEER_ROWS), array(128 * BLOCK...  6.48 us
    ppermute x2, waiting for transfers between devices, swapped(): far = lax.ppermute(far, axis, list(enumerate(apart)))  5.8 us
    pallas_call x1, Pallas kernels, body(): call(load_kernel, [SMEM] + geometry_specs + [VMEM] * 3, [array(3 * 1024),...  5.31 us
    ppermute x2, starting transfers between devices, swapped(): far = lax.ppermute(far, axis, list(enumerate(apart)))  4.12 us
    pallas_call x1, Pallas kernels, body(): call(final_kernel, geometry_specs + [VMEM] * 4, [array(3 * 1024), array(1...  2.17 us
    ppermute x2, starting transfers between devices, swapped(): return (lax.ppermute(near, axis, [(i, i ^ 1) for i in range(count)]), far)  2.06 us
  transfers between devices with their start and end apart: 4, of which 2 were waited for; matrix products, arithmetic and copies ran while one was open for 0% of the time, Pallas kernels for 0%

profile of v4, /device:TPU:1, one launch (start us, length us, event | category | flops | bytes accessed | tf_op | source)
XLA Modules:
  0.0 70.6 jit_solution(10025864983912674252)
XLA Ops:
  0.6 6.5 %pack.1 = (f32[1792,128]{1,0:T(8,128)}, f32[3072,128]{1,0:T(8,128)}) custom-call(s32[128]{0:T(128)} %ids.1, f32[128]{0:T(128)} %len_axial.5, f32[16]{0:T(128)} %len_azim.5, f32[1,128]{1,0:T(1,128)} %bitcast.15, f32[576,2048]{1,0:T(8,128)} %bitcast.19), custom_call_target="tpu_custom_call" | custom-call | tf_op jit(solution)/shard_map/pack/pallas_call | solution.py:698
  7.1 0.0 copy-start
  7.1 0.0 copy-start.1
  7.1 0.0 copy-start.2
  7.2 0.0 copy-start.3
  7.2 0.0 copy-start.4
  7.2 0.0 copy-start.5
  7.2 25.5 %all_to_all.10 = f32[32,56,128]{2,1,0:T(8,128)S(1)} all-to-all(f32[32,56,128]{2,1,0:T(8,128)} %bitcast.20), channel_id=1, replica_groups=mesh['stream'=32,'azim'=4] {'stream'}, dimensions={0} | all-to-all | bytes 1835008 | tf_op jit(solution)/shard_map/all_to_all | solution.py:721
  32.7 0.0 copy-done
  32.7 0.0 copy-done.1
  32.7 0.0 copy-done.2
  32.7 0.0 copy-done.3
  32.7 0.0 copy-done.4
  32.7 0.0 copy-done.5
  32.7 5.3 %load.1 = (f32[3072,128]{1,0:T(8,128)S(1)}, f32[1024,128]{1,0:T(8,128)S(1)}, f32[128,128]{1,0:T(8,128)S(1)}, f32[128,128]{1,0:T(8,128)S(1)}) custom-call(s32[128]{0:T(128)S(1)} %copy-done.5, f32[128]{0:T(128)S(1)} %copy-done.2, f32[16]{0:T(128)S(1)} %copy-done.3, f32[1,128]{1,0:T(1,128)S(1)} %bitcast.16, s32[16,128]{1,0:T(8,128)S(1)} %bitcast.14, ...), custom_call_target="tpu_custom_call" | custom-call | tf_op jit(solution)/shard_map/load/pallas_call | solution.py:724
  38.1 0.5 collective-permute-start
  38.5 2.3 %collective-permute-start.1 = (f32[128,128]{1,0:T(8,128)S(1)}, f32[128,128]{1,0:T(8,128)S(1)}, u32[]{:S(2)}, u32[]{:S(2)}) collective-permute-start(f32[128,128]{1,0:T(8,128)S(1)} %get-tuple-element.21), channel_id=1, source_target_pairs={{0,0},{4,8},{8,4},{12,16},{16,12},{20,24},{24,20},{28,32},{32,28},... | collective-permute-start | bytes 196616 | tf_op jit(solution)/shard_map/ppermute | solution.py:688
  40.8 0.0 collective-permute-done.near_in
  40.9 3.2 %collective-permute-done.1.far_in = f32[128,128]{1,0:T(8,128)S(1)} collective-permute-done((f32[128,128]{1,0:T(8,128)S(1)}, f32[128,128]{1,0:T(8,128)S(1)}, u32[]{:S(2)}, u32[]{:S(2)}) %collective-permute-start.1) | collective-permute-done | bytes 65568 | tf_op jit(solution)/shard_map/ppermute | solution.py:688
  44.1 0.1 axial_faces.1
  44.3 1.6 %collective-permute-start.2 = (f32[136,128]{1,0:T(8,128)S(1)}, f32[136,128]{1,0:T(8,128)S(1)}, u32[]{:S(2)}, u32[]{:S(2)}) collective-permute-start(f32[136,128]{1,0:T(8,128)S(1)} %get-tuple-element.24), channel_id=1, source_target_pairs={{0,1},{1,0},{2,3},{3,2},{4,5},{5,4},{6,7},{7,6},{8,9},{9,8},{10,11... | collective-permute-start | bytes 208904 | tf_op jit(solution)/shard_map/ppermute | solution.py:689
  45.8 1.8 %collective-permute-start.3 = (f32[136,128]{1,0:T(8,128)S(1)}, f32[136,128]{1,0:T(8,128)S(1)}, u32[]{:S(2)}, u32[]{:S(2)}) collective-permute-start(f32[136,128]{1,0:T(8,128)S(1)} %get-tuple-element.25), channel_id=1, source_target_pairs={{0,3},{1,2},{2,1},{3,0},{4,7},{5,6},{6,5},{7,4},{8,11},{9,10},{10,... | collective-permute-start | bytes 208904 | tf_op jit(solution)/shard_map/ppermute | solution.py:688
  47.7 0.0 collective-permute-done.2.near
  47.7 2.5 %collective-permute-done.3.far = f32[136,128]{1,0:T(8,128)S(1)} collective-permute-done((f32[136,128]{1,0:T(8,128)S(1)}, f32[136,128]{1,0:T(8,128)S(1)}, u32[]{:S(2)}, u32[]{:S(2)}) %collective-permute-start.3) | collective-permute-done | bytes 69664 | tf_op jit(solution)/shard_map/ppermute | solution.py:688
  50.2 1.7 %image.1 = (f32[1024,128]{1,0:T(8,128)S(1)}, f32[1024,128]{1,0:T(8,128)S(1)}, f32[128,128]{1,0:T(8,128)S(1)}) custom-call(f32[128]{0:T(128)S(1)} %copy-done.2, f32[16]{0:T(128)S(1)} %copy-done.3, f32[1,128]{1,0:T(1,128)S(1)} %bitcast.17, f32[1024,128]{1,0:T(8,128)S(1)} %get-tuple-element.22.part, f32[128,128]{1,0:T(8,128)S(1)} %get-tuple-element.23.normals_in, ...), custom_call_target="tpu_custom_call" | custom-call | tf_op jit(solution)/shard_map/image/pallas_call | solution.py:745
  51.9 16.6 %all_to_all.11 = f32[128,1,128]{2,1,0:T(1,128)S(1)} all-to-all(f32[128,1,128]{2,1,0:T(1,128)S(1)} %bitcast.13), channel_id=1, replica_groups=mesh['stream'=32,'azim'=4] {'stream','azim'}, dimensions={0} | all-to-all | bytes 131072 | tf_op jit(solution)/shard_map/all_to_all | solution.py:752
  68.5 2.2 %velocity.1 = (f32[3072,128]{1,0:T(8,128)}, f32[1024,128]{1,0:T(8,128)}) custom-call(f32[128]{0:T(128)S(1)} %copy-done.2, f32[16]{0:T(128)S(1)} %copy-done.3, f32[1,128]{1,0:T(1,128)S(1)} %bitcast.18, f32[128,128]{1,0:T(8,128)S(1)} %bitcast.12, f32[1024,128]{1,0:T(8,128)S(1)} %get-tuple-element.27.field, f32[1024,128]{1,0:T(8,128)S(1)} %get-tuple-element.28.image, ...), custom_call_target="tpu_custom_call" | custom-call | tf_op jit(solution)/shard_map/velocity/pallas_call | solution.py:759
Async XLA Ops:
  7.1 25.6 %copy-start = (f32[3072,128]{1,0:T(8,128)S(1)}, f32[3072,128]{1,0:T(8,128)}, u32[]{:S(2)}) copy-start(f32[3072,128]{1,0:T(8,128)} %get-tuple-element.18.keep) | copy-start | bytes 4718596
  7.1 25.6 %copy-start.1 = (s32[4,4,128]{2,1,0:T(4,128)S(1)}, s32[4,4,128]{2,1,0:T(4,128)}, u32[]{:S(2)}) copy-start(s32[4,4,128]{2,1,0:T(4,128)} %param.11) | copy-start | bytes 24580
  7.1 25.6 %copy-start.2 = (f32[128]{0:T(128)S(1)}, f32[128]{0:T(128)}, u32[]{:S(2)}) copy-start(f32[128]{0:T(128)} %len_axial.5) | copy-start | bytes 1540
  7.2 25.6 %copy-start.3 = (f32[16]{0:T(128)S(1)}, f32[16]{0:T(128)}, u32[]{:S(2)}) copy-start(f32[16]{0:T(128)} %len_azim.5) | copy-start | bytes 196
  7.2 25.6 %copy-start.4 = (f32[128]{0:T(128)S(1)}, f32[128]{0:T(128)}, u32[]{:S(2)}) copy-start(f32[128]{0:T(128)} %param.10) | copy-start | bytes 1540
  7.2 25.6 %copy-start.5 = (s32[128]{0:T(128)S(1)}, s32[128]{0:T(128)}, u32[]{:S(2)}) copy-start(s32[128]{0:T(128)} %ids.1) | copy-start | bytes 1540
  38.1 2.8 %collective-permute-start = (f32[128,128]{1,0:T(8,128)S(1)}, f32[128,128]{1,0:T(8,128)S(1)}, u32[]{:S(2)}, u32[]{:S(2)}) collective-permute-start(f32[128,128]{1,0:T(8,128)S(1)} %get-tuple-element.20), channel_id=1, source_target_pairs={{0,4},{4,0},{8,12},{12,8},{16,20},{20,16},{24,28},{28,24},{32,36},... | collective-permute-start | bytes 196616 | tf_op jit(solution)/shard_map/ppermute | solution.py:689
  38.5 5.6 %collective-permute-start.1 = (f32[128,128]{1,0:T(8,128)S(1)}, f32[128,128]{1,0:T(8,128)S(1)}, u32[]{:S(2)}, u32[]{:S(2)}) collective-permute-start(f32[128,128]{1,0:T(8,128)S(1)} %get-tuple-element.21), channel_id=1, source_target_pairs={{0,0},{4,8},{8,4},{12,16},{16,12},{20,24},{24,20},{28,32},{32,28},... | collective-permute-start | bytes 196616 | tf_op jit(solution)/shard_map/ppermute | solution.py:688
  44.3 3.4 %collective-permute-start.2 = (f32[136,128]{1,0:T(8,128)S(1)}, f32[136,128]{1,0:T(8,128)S(1)}, u32[]{:S(2)}, u32[]{:S(2)}) collective-permute-start(f32[136,128]{1,0:T(8,128)S(1)} %get-tuple-element.24), channel_id=1, source_target_pairs={{0,1},{1,0},{2,3},{3,2},{4,5},{5,4},{6,7},{7,6},{8,9},{9,8},{10,11... | collective-permute-start | bytes 208904 | tf_op jit(solution)/shard_map/ppermute | solution.py:689
  45.8 4.4 %collective-permute-start.3 = (f32[136,128]{1,0:T(8,128)S(1)}, f32[136,128]{1,0:T(8,128)S(1)}, u32[]{:S(2)}, u32[]{:S(2)}) collective-permute-start(f32[136,128]{1,0:T(8,128)S(1)} %get-tuple-element.25), channel_id=1, source_target_pairs={{0,3},{1,2},{2,1},{3,0},{4,7},{5,6},{6,5},{7,4},{8,11},{9,10},{10,... | collective-permute-start | bytes 208904 | tf_op jit(solution)/shard_map/ppermute | solution.py:688

commit v5 on v3

--- a/solution.py
+++ b/solution.py
@@ -349,7 +349,7 @@
                 pred[pl.ds(comp * 1024 + 8 * t * 16 + j, ROWS, stride=16), :] = tile
         return carry
 
-    lax.fori_loop(0, 16, unpack, 0, unroll=4)
+    lax.fori_loop(0, 16, unpack, 0, unroll=2)
 
     axial, azim, radial, _ = lengths(len_axial, len_azim, len_radial, sub)
     inverse = [

time: 69.8 us -> 69.6 us (level)
  no operation moved by 1% of the time
where the time goes in v5:
time: 69.6 us; the launch traced here: 69.3 us
  blocking collectives  42.1 us (60%)
  Pallas kernels  14.5 us (21%)
  starting transfers between devices  6.18 us (9%)
  waiting for transfers between devices  5.81 us (8%)
  between operations  0.74 us (1%)
    all_to_all x1, blocking collectives, body(): lax.all_to_all(send.reshape(slabs, PEER_ROWS, 128), 'stream', split_axis=...  25.5 us
    all_to_all x1, blocking collectives, body(): lax.all_to_all(sums.reshape(slabs * sectors, 1, 128), ('stream', 'azim'),...  16.6 us
    pallas_call x1, Pallas kernels, body(): call(pack_kernel, [HBM] * 5, [array(slabs * PEER_ROWS), array(128 * BLOCK...  6.48 us
    ppermute x2, waiting for transfers between devices, swapped(): far = lax.ppermute(far, axis, list(enumerate(apart)))  5.8 us
    ppermute x2, starting transfers between devices, swapped(): far = lax.ppermute(far, axis, list(enumerate(apart)))  4.12 us
    pallas_call x1, Pallas kernels, body(): call(load_kernel, [SMEM] + geometry_specs + [VMEM] * 3, [array(3 * 1024),...  4.07 us
    pallas_call x1, Pallas kernels, body(): call(final_kernel, geometry_specs + [VMEM] * 4, [array(3 * 1024), array(1...  2.09 us
    ppermute x2, starting transfers between devices, swapped(): return (lax.ppermute(near, axis, [(i, i ^ 1) for i in range(count)]), far)  2.06 us
  transfers between devices with their start and end apart: 4, of which 2 were waited for; matrix products, arithmetic and copies ran while one was open for 0% of the time, Pallas kernels for 0%

profile of v5, /device:TPU:1, one launch (start us, length us, event | category | flops | bytes accessed | tf_op | source)
XLA Modules:
  0.0 69.3 jit_solution(7558974311519795182)
XLA Ops:
  0.6 6.5 %pack.1 = (f32[1792,128]{1,0:T(8,128)}, f32[3072,128]{1,0:T(8,128)}) custom-call(s32[128]{0:T(128)} %ids.1, f32[128]{0:T(128)} %len_axial.5, f32[16]{0:T(128)} %len_azim.5, f32[1,128]{1,0:T(1,128)} %bitcast.15, f32[576,2048]{1,0:T(8,128)} %bitcast.19), custom_call_target="tpu_custom_call" | custom-call | tf_op jit(solution)/shard_map/pack/pallas_call | solution.py:685
  7.1 0.0 copy-start
  7.1 0.0 copy-start.1
  7.1 0.0 copy-start.2
  7.2 0.0 copy-start.3
  7.2 0.0 copy-start.4
  7.2 0.0 copy-start.5
  7.2 25.5 %all_to_all.10 = f32[32,56,128]{2,1,0:T(8,128)S(1)} all-to-all(f32[32,56,128]{2,1,0:T(8,128)} %bitcast.20), channel_id=1, replica_groups=mesh['stream'=32,'azim'=4] {'stream'}, dimensions={0} | all-to-all | bytes 1835008 | tf_op jit(solution)/shard_map/all_to_all | solution.py:708
  32.7 0.0 copy-done
  32.7 0.0 copy-done.1
  32.7 0.0 copy-done.2
  32.7 0.0 copy-done.3
  32.7 0.0 copy-done.4
  32.7 0.0 copy-done.5
  32.7 4.1 %load.1 = (f32[3072,128]{1,0:T(8,128)S(1)}, f32[1024,128]{1,0:T(8,128)S(1)}, f32[128,128]{1,0:T(8,128)S(1)}, f32[128,128]{1,0:T(8,128)S(1)}) custom-call(s32[128]{0:T(128)S(1)} %copy-done.5, f32[128]{0:T(128)S(1)} %copy-done.2, f32[16]{0:T(128)S(1)} %copy-done.3, f32[1,128]{1,0:T(1,128)S(1)} %bitcast.16, s32[16,128]{1,0:T(8,128)S(1)} %bitcast.14, ...), custom_call_target="tpu_custom_call" | custom-call | tf_op jit(solution)/shard_map/load/pallas_call | solution.py:711
  36.8 0.5 collective-permute-start
  37.3 2.3 %collective-permute-start.1 = (f32[128,128]{1,0:T(8,128)S(1)}, f32[128,128]{1,0:T(8,128)S(1)}, u32[]{:S(2)}, u32[]{:S(2)}) collective-permute-start(f32[128,128]{1,0:T(8,128)S(1)} %get-tuple-element.21), channel_id=1, source_target_pairs={{0,0},{4,8},{8,4},{12,16},{16,12},{20,24},{24,20},{28,32},{32,28},... | collective-permute-start | bytes 196616 | tf_op jit(solution)/shard_map/ppermute | solution.py:675
  39.6 0.0 collective-permute-done.near_in
  39.6 3.2 %collective-permute-done.1.far_in = f32[128,128]{1,0:T(8,128)S(1)} collective-permute-done((f32[128,128]{1,0:T(8,128)S(1)}, f32[128,128]{1,0:T(8,128)S(1)}, u32[]{:S(2)}, u32[]{:S(2)}) %collective-permute-start.1) | collective-permute-done | bytes 65568 | tf_op jit(solution)/shard_map/ppermute | solution.py:675
  42.9 0.1 axial_faces.1
  43.0 1.6 %collective-permute-start.2 = (f32[136,128]{1,0:T(8,128)S(1)}, f32[136,128]{1,0:T(8,128)S(1)}, u32[]{:S(2)}, u32[]{:S(2)}) collective-permute-start(f32[136,128]{1,0:T(8,128)S(1)} %get-tuple-element.24), channel_id=1, source_target_pairs={{0,1},{1,0},{2,3},{3,2},{4,5},{5,4},{6,7},{7,6},{8,9},{9,8},{10,11... | collective-permute-start | bytes 208904 | tf_op jit(solution)/shard_map/ppermute | solution.py:676
  44.6 1.8 %collective-permute-start.3 = (f32[136,128]{1,0:T(8,128)S(1)}, f32[136,128]{1,0:T(8,128)S(1)}, u32[]{:S(2)}, u32[]{:S(2)}) collective-permute-start(f32[136,128]{1,0:T(8,128)S(1)} %get-tuple-element.25), channel_id=1, source_target_pairs={{0,3},{1,2},{2,1},{3,0},{4,7},{5,6},{6,5},{7,4},{8,11},{9,10},{10,... | collective-permute-start | bytes 208904 | tf_op jit(solution)/shard_map/ppermute | solution.py:675
  46.4 0.0 collective-permute-done.2.near
  46.4 2.6 %collective-permute-done.3.far = f32[136,128]{1,0:T(8,128)S(1)} collective-permute-done((f32[136,128]{1,0:T(8,128)S(1)}, f32[136,128]{1,0:T(8,128)S(1)}, u32[]{:S(2)}, u32[]{:S(2)}) %collective-permute-start.3) | collective-permute-done | bytes 69664 | tf_op jit(solution)/shard_map/ppermute | solution.py:675
  49.0 1.7 %image.1 = (f32[1024,128]{1,0:T(8,128)S(1)}, f32[1024,128]{1,0:T(8,128)S(1)}, f32[128,128]{1,0:T(8,128)S(1)}) custom-call(f32[128]{0:T(128)S(1)} %copy-done.2, f32[16]{0:T(128)S(1)} %copy-done.3, f32[1,128]{1,0:T(1,128)S(1)} %bitcast.17, f32[1024,128]{1,0:T(8,128)S(1)} %get-tuple-element.22.part, f32[128,128]{1,0:T(8,128)S(1)} %get-tuple-element.23.normals_in, ...), custom_call_target="tpu_custom_call" | custom-call | tf_op jit(solution)/shard_map/image/pallas_call | solution.py:732
  50.6 16.6 %all_to_all.11 = f32[128,1,128]{2,1,0:T(1,128)S(1)} all-to-all(f32[128,1,128]{2,1,0:T(1,128)S(1)} %bitcast.13), channel_id=1, replica_groups=mesh['stream'=32,'azim'=4] {'stream','azim'}, dimensions={0} | all-to-all | bytes 131072 | tf_op jit(solution)/shard_map/all_to_all | solution.py:739
  67.2 2.1 %velocity.1 = (f32[3072,128]{1,0:T(8,128)}, f32[1024,128]{1,0:T(8,128)}) custom-call(f32[128]{0:T(128)S(1)} %copy-done.2, f32[16]{0:T(128)S(1)} %copy-done.3, f32[1,128]{1,0:T(1,128)S(1)} %bitcast.18, f32[128,128]{1,0:T(8,128)S(1)} %bitcast.12, f32[1024,128]{1,0:T(8,128)S(1)} %get-tuple-element.27.field, f32[1024,128]{1,0:T(8,128)S(1)} %get-tuple-element.28.image, ...), custom_call_target="tpu_custom_call" | custom-call | tf_op jit(solution)/shard_map/velocity/pallas_call | solution.py:746
Async XLA Ops:
  7.1 25.6 %copy-start = (f32[3072,128]{1,0:T(8,128)S(1)}, f32[3072,128]{1,0:T(8,128)}, u32[]{:S(2)}) copy-start(f32[3072,128]{1,0:T(8,128)} %get-tuple-element.18.keep) | copy-start | bytes 4718596
  7.1 25.6 %copy-start.1 = (s32[4,4,128]{2,1,0:T(4,128)S(1)}, s32[4,4,128]{2,1,0:T(4,128)}, u32[]{:S(2)}) copy-start(s32[4,4,128]{2,1,0:T(4,128)} %param.11) | copy-start | bytes 24580
  7.1 25.6 %copy-start.2 = (f32[128]{0:T(128)S(1)}, f32[128]{0:T(128)}, u32[]{:S(2)}) copy-start(f32[128]{0:T(128)} %len_axial.5) | copy-start | bytes 1540
  7.2 25.6 %copy-start.3 = (f32[16]{0:T(128)S(1)}, f32[16]{0:T(128)}, u32[]{:S(2)}) copy-start(f32[16]{0:T(128)} %len_azim.5) | copy-start | bytes 196
  7.2 25.6 %copy-start.4 = (f32[128]{0:T(128)S(1)}, f32[128]{0:T(128)}, u32[]{:S(2)}) copy-start(f32[128]{0:T(128)} %param.10) | copy-start | bytes 1540
  7.2 25.6 %copy-start.5 = (s32[128]{0:T(128)S(1)}, s32[128]{0:T(128)}, u32[]{:S(2)}) copy-start(s32[128]{0:T(128)} %ids.1) | copy-start | bytes 1540
  36.8 2.8 %collective-permute-start = (f32[128,128]{1,0:T(8,128)S(1)}, f32[128,128]{1,0:T(8,128)S(1)}, u32[]{:S(2)}, u32[]{:S(2)}) collective-permute-start(f32[128,128]{1,0:T(8,128)S(1)} %get-tuple-element.20), channel_id=1, source_target_pairs={{0,4},{4,0},{8,12},{12,8},{16,20},{20,16},{24,28},{28,24},{32,36},... | collective-permute-start | bytes 196616 | tf_op jit(solution)/shard_map/ppermute | solution.py:676
  37.3 5.6 %collective-permute-start.1 = (f32[128,128]{1,0:T(8,128)S(1)}, f32[128,128]{1,0:T(8,128)S(1)}, u32[]{:S(2)}, u32[]{:S(2)}) collective-permute-start(f32[128,128]{1,0:T(8,128)S(1)} %get-tuple-element.21), channel_id=1, source_target_pairs={{0,0},{4,8},{8,4},{12,16},{16,12},{20,24},{24,20},{28,32},{32,28},... | collective-permute-start | bytes 196616 | tf_op jit(solution)/shard_map/ppermute | solution.py:675
  43.0 3.4 %collective-permute-start.2 = (f32[136,128]{1,0:T(8,128)S(1)}, f32[136,128]{1,0:T(8,128)S(1)}, u32[]{:S(2)}, u32[]{:S(2)}) collective-permute-start(f32[136,128]{1,0:T(8,128)S(1)} %get-tuple-element.24), channel_id=1, source_target_pairs={{0,1},{1,0},{2,3},{3,2},{4,5},{5,4},{6,7},{7,6},{8,9},{9,8},{10,11... | collective-permute-start | bytes 208904 | tf_op jit(solution)/shard_map/ppermute | solution.py:676
  44.6 4.4 %collective-permute-start.3 = (f32[136,128]{1,0:T(8,128)S(1)}, f32[136,128]{1,0:T(8,128)S(1)}, u32[]{:S(2)}, u32[]{:S(2)}) collective-permute-start(f32[136,128]{1,0:T(8,128)S(1)} %get-tuple-element.25), channel_id=1, source_target_pairs={{0,3},{1,2},{2,1},{3,0},{4,7},{5,6},{6,5},{7,4},{8,11},{9,10},{10,... | collective-permute-start | bytes 208904 | tf_op jit(solution)/shard_map/ppermute | solution.py:675
